TPU v7x, 32 devices: a whole 2x2x4 slice. The times are simulated.
32 devices in a mesh: op: 4 (over y, core), lsec: 2 (over x), rsec: 4 (over z).
Axes of the slice: x: 2, y: 2, z: 4, core: 2. Of those that a mesh axis runs over, the one named last changes fastest.
Arguments:
- wavefn: float32 [8, 16, 128, 128], P('lsec', 'rsec'), may hold values from -6 to 6
- left_ops: float32 [28, 8, 128, 128], P('op', 'lsec'), may hold values from -0.5 to 0.5
- right_ops: float32 [28, 16, 128, 128], P('op', 'rsec'), may hold values from -0.09375 to 0.09375
- term_shift: int32 [28], P('op'), may hold values from 0 to 1
Outputs:
- sigma: float32 [8, 16, 128, 128], P('lsec', 'rsec', 'op')
All inputs are finite; a program needn't handle non-finite values.
Results may differ from a plain program's by a relative error of at most 0.0001.
Values sent between devices are 32-bit elements; how exact they have to be, the bound alone decides.
No kernel may reach another device: no remote copies, remote signals or barrier semaphores. Data moves between devices by JAX's collectives and lax.ppermute only.
A program may use at most 64 MiB of HBM per device.

v0:
```python
import functools

import jax
import jax.numpy as jnp
from jax import lax
from jax.experimental import pallas as pl
from jax.experimental.pallas import tpu as pltpu
from jax.sharding import PartitionSpec as P

WIDTHS = (2, 2)
CORES = 2
ARRANGE_COST = 1
ADD_COST = 2 * 10 ** 9
LANDED_COST = 6 * 10 ** 8
LIMIT = 32 * 1024 * 1024
NT = (((1,), (1,)), ((), ()))
PARAMS = pltpu.CompilerParams(vmem_limit_bytes=LIMIT)
HBM = pl.BlockSpec(memory_space=pltpu.HBM)
VMEM = pl.BlockSpec(memory_space=pltpu.VMEM)
ANY = pl.BlockSpec(memory_space=pl.ANY)


def split(value):
    high = value.astype(jnp.bfloat16)
    low = (value - high.astype(jnp.float32)).astype(jnp.bfloat16)
    return high, low


def choose_rows(lops, left, l):
    terms, _, many, _ = lops.shape
    for t in range(terms):
        left[l, t * many:(t + 1) * many, :] = jnp.concatenate(split(lops[t, l]), axis=1)


def lines(many, rows, slots, second):
    core = lax.rem(lax.axis_index("op"), CORES)
    return core * (rows // 8), (1 - core) * (rows // 8), skipped(slots, second) * (many // 8)


def products(left, psi, right, chosen, inner, total, send, keep, start, begins, lops=None, rops=None, ready=()):
    slots, height, twice = left.shape
    size = twice // 2
    wide, terms = right.shape[:2]
    many = height // terms
    chips, blocks, rows, _ = keep.shape
    second = blocks // wide - slots
    here, there, skip = begins
    for r in range(wide):
        for l in range(slots):
            if r == 0 and lops is not None:
                choose_rows(lops, left, l)
            both = jnp.concatenate(split(psi[l, start + r]), axis=1)
            out = jnp.dot(left[l], jnp.concatenate([both, both], axis=0), preferred_element_type=jnp.float32)
            for t in range(terms):
                block = out[t * many:(t + 1) * many]
                parts = split(block[:, :size] + block[:, size:])
                inner[t, l * many:(l + 1) * many, :] = jnp.concatenate(parts, axis=1)
        if r == 0:
            for copy in ready:
                copy.wait()
        for t in range(terms):
            if rops is not None:
                right[r, t] = jnp.concatenate(split(rops[t, r]), axis=0)
            both = right[r, t]
            out = lax.dot_general(
                inner[t], jnp.concatenate([both, both], axis=1), NT, preferred_element_type=jnp.float32
            )
            out = (out[:, :size] + out[:, size:]).reshape(-1, 8, size)
            for way in range(2):
                mine = out * chosen[t, way]
                total[way] = mine if t == 0 else total[way] + mine
        for chip in range(chips):
            for at in range(slots + second):
                way = 0 if at < slots else 1
                l = at if at < slots else at - slots
                for ref, begin in ((keep, here), (send, there)):
                    line = begin + (l * many + chip * CORES * rows) // 8 + (skip if way else 0)
                    block = total[way, pl.ds(line, rows // 8)].reshape(rows, size)
                    if isinstance(ref, (list, tuple)):
                        ref[r][chip, at] = block
                    else:
                        ref[chip, at * wide + r] = block


def skipped(slots, second):
    return 0 if second == slots else 1 - lax.axis_index("lsec")


def first_others(shift, psi, lops, rops, send, keep, left, right, chosen, lops_own, psi_all, rops_rest, *refs):
    bits, lops_now, rops_now, inner, total, sems, lsems = refs
    terms, slots, size, _ = lops.shape
    wide = right.shape[0]
    ny = lax.axis_size("op") // CORES
    mine = lax.div(lax.axis_index("op"), CORES)
    share = size // ny

    def rows(ahead, target):
        at = pl.multiple_of(lax.rem(mine + ahead, ny) * share, share)
        return pltpu.make_async_copy(lops.at[:, :, pl.ds(at, share)], target, lsems.at[ahead])

    copies = [rows(ahead, lops_now.at[:, :, pl.ds((ahead - 1) * share, share)]) for ahead in range(1, ny)] + [
        pltpu.make_async_copy(psi.at[:, :wide], psi_all.at[:, :wide], sems.at[0]),
        pltpu.make_async_copy(shift, bits, sems.at[1]),
    ]
    ready = [pltpu.make_async_copy(rops.at[:, :wide], rops_now, sems.at[2])]
    later = [rows(0, lops_own)]
    if wide < rops.shape[1]:
        later += [
            pltpu.make_async_copy(psi.at[:, wide:], psi_all.at[:, wide:], sems.at[3]),
            pltpu.make_async_copy(rops.at[:, wide:], rops_rest, sems.at[4]),
        ]
    for copy in copies + ready:
        copy.start()
    second = keep.shape[1] // wide - slots
    begins = lines(lops_now.shape[2], keep.shape[2], slots, second)
    flip = lax.axis_index("lsec") if second < slots else 0
    for copy in copies:
        copy.wait()
    for copy in later:
        copy.start()
    for t in range(terms):
        kept = jnp.where(flip == 1, 1 - bits[t], bits[t]).astype(jnp.float32)
        chosen[t, 0] = jnp.full((8, size), kept, jnp.float32)
        chosen[t, 1] = jnp.full((8, size), 1.0 - kept, jnp.float32)
    products(
        left, psi_all, right, chosen, inner, total, send, keep, 0, begins, lops_now, rops_now, ready
    )
    for copy in later:
        copy.wait()


def find(left, keep, right):
    slots, height, _ = left.shape
    wide, terms = right.shape[:2]
    return lines(height // terms, keep.shape[2], slots, keep.shape[1] // wide - slots)


def first_own(lops, psi, right, chosen, send, keep, left, inner, total):
    products(left, psi, right, chosen, inner, total, send, keep, 0, find(left, keep, right), lops)


def later_others(start, skip, left, psi, rops, chosen, after, *refs):
    wide = refs[-3].shape[0]
    send, (keep, right, inner, total) = refs[:wide], refs[wide:]
    products(
        left, psi, right, chosen, inner, total, send, keep, start, find(left, keep, right),
        rops=rops.at[:, start - skip:],
    )


def later_own(start, left, psi, right, chosen, after, send, keep, inner, total):
    products(left, psi, right, chosen, inner, total, send, keep, start, find(left, keep, right))


def call(kernel, operands, in_specs, out_shape, scratch=(), flops=1):
    return pl.pallas_call(
        kernel,
        in_specs=in_specs,
        out_specs=[VMEM] * len(out_shape),
        out_shape=out_shape,
        scratch_shapes=scratch,
        compiler_params=PARAMS,
        cost_estimate=pl.CostEstimate(flops=flops, bytes_accessed=1024, transcendentals=0),
    )(*operands)


def sums(kernel, shapes, operands, after=None, flops=1):
    reads = len(operands)
    specs = [VMEM] * reads

    def body(*refs):
        kernel(refs[:reads], refs[len(specs):])

    if after is not None:
        operands = [*operands, after]
        specs.append(ANY)
    return call(body, operands, specs, [jax.ShapeDtypeStruct(shape, jnp.float32) for shape in shapes], (), flops)


def arrange(slots, first, second):
    wide, rows, size = first.shape[1:]
    more = second.shape[0]

    def kernel(refs, outs):
        way = 1 - lax.axis_index("lsec") if more < slots else 0
        skip = 1 - skipped(slots, more) if more < slots else 0
        for l in range(slots):
            outs[0][way, l] = refs[0][l]
        for j in range(more):
            outs[0][1 - way, j + skip] = refs[1][j]

    return sums(kernel, [(2, slots, wide, rows, size)], [first, second], None, ARRANGE_COST)[0]


def settle(arranged, first, second):
    slots = first.shape[0]
    rows, size = first.shape[2:]
    more = second.shape[0]
    widths = [value.shape[2] for value in arranged] + [first.shape[1]]
    across = sum(widths)
    n_left, n_right = lax.axis_size("lsec"), lax.axis_size("rsec")

    def kernel(*refs):
        out, every = refs[-2:]
        mine_l, mine_r = lax.axis_index("lsec"), lax.axis_index("rsec")
        first_l, last_l = (mine_l == 0).astype(jnp.int32), (mine_l == n_left - 1).astype(jnp.int32)
        first_r, last_r = (mine_r == 0).astype(jnp.int32), (mine_r == n_right - 1).astype(jnp.int32)
        steps = ((first_l, -last_r), (-last_l, first_r))
        start = 0
        for i, wide in enumerate(widths[:-1]):
            every[:, :, start:start + wide] = refs[i][...]
            start += wide
        way = 1 - mine_l if more < slots else 0
        skip = 1 - skipped(slots, more) if more < slots else 0
        a, b = refs[len(arranged):len(arranged) + 2]
        for l in range(slots):
            every[way, l, start:] = a[l]
        for j in range(more):
            every[1 - way, j + skip, start:] = b[j]
        for l in range(slots):
            for r in range(across):
                block = jnp.zeros((rows, size), jnp.float32)
                for side, (step_l, step_r) in enumerate(steps):
                    from_l, from_r = l - step_l, r - step_r
                    inside = (from_l >= 0) & (from_l < slots) & (from_r >= 0) & (from_r < across)
                    part = every[side, jnp.clip(from_l, 0, slots - 1), jnp.clip(from_r, 0, across - 1)]
                    block = block + jnp.where(inside, part, 0.0)
                out[l, r] = block

    operands = [*arranged, first, second]
    return call(
        kernel, operands, [VMEM] * len(operands),
        [jax.ShapeDtypeStruct((slots, across, rows, size), jnp.float32)],
        [pltpu.VMEM((2, slots, across, rows, size), jnp.float32)],
    )[0]


def shards(wavefn, left_ops, right_ops, term_shift):
    n_op, n_left, n_right = (lax.axis_size(axis) for axis in ("op", "lsec", "rsec"))
    across = wavefn.shape[1]
    terms, slots, size, _ = left_ops.shape
    ny = n_op // CORES
    share = size // ny
    others = (ny - 1) * share
    rows = size // n_op
    second = slots - 1 if n_left == 2 else slots
    f32, bf16 = jnp.float32, jnp.bfloat16

    def permute(value, target):
        def place(o, l, r):
            return (o % n_op * n_left + l % n_left) * n_right + r % n_right

        perm = [
            (place(o, l, r), place(*target(o, l, r)))
            for o in range(n_op) for l in range(n_left) for r in range(n_right)
        ]
        return lax.ppermute(value, ("op", "lsec", "rsec"), perm)

    def swap(value):
        return permute(value, lambda o, l, r: (o ^ 1, l, r))

    def ahead(value, by):
        return permute(value, lambda o, l, r: (o + CORES * by, l, r))

    def sectors(value, way):
        def target(o, l, r):
            up = way == (l if second < slots else 0)
            return (o, l + 1, r - 1) if up else (o, l - 1, r + 1)

        return permute(value, target)

    def blocks(wide):
        return (slots + second) * wide

    def result(chips, wide):
        return jax.ShapeDtypeStruct((chips, blocks(wide), rows, size), f32)

    def work(many):
        return [
            pltpu.VMEM((terms, slots * many, 2 * size), bf16),
            pltpu.VMEM((2, slots * many // 8, 8, size), f32),
        ]

    def add_cores(refs, outs):
        for at, out in enumerate(outs):
            if len(refs) == 2:
                out[...] = refs[0][at] + refs[1][at]
            else:
                wide = len(refs) - 1
                for block in range(out.shape[0]):
                    out[block] = refs[0][at, block] + refs[1 + block % wide][at, block // wide]

    def add_all(refs, outs):
        total = refs[0][...]
        for ref in refs[1:]:
            total = total + ref[...].reshape(total.shape)
        total = total.reshape(-1, rows, size)
        start = 0
        for out in outs:
            count = 1
            for length in out.shape[:-2]:
                count *= length
            out[...] = total[start:start + count].reshape(out.shape)
            start += count

    def landed_first(refs, outs):
        outs[0][...] = refs[0][...]

    widths = WIDTHS if sum(WIDTHS) == across else (across,)
    starts = [sum(widths[:i]) for i in range(len(widths))]
    count = len(widths)
    pieces, own_kept, own_arrived, arrived, kept = [], [], [], [], []

    arguments = (term_shift, wavefn, left_ops, right_ops)
    wide = widths[0]
    send, keep, left, right, chosen, lops, psi, rops = call(
        first_others,
        [pltpu.with_memory_space_constraint(value, pltpu.HBM) for value in arguments],
        [HBM] * 4,
        [result(ny - 1, wide)] * 2 + [
            jax.ShapeDtypeStruct((slots, terms * others, 2 * size), bf16),
            jax.ShapeDtypeStruct((wide, terms, 2 * size, size), bf16),
            jax.ShapeDtypeStruct((terms, 2, 8, size), f32),
            jax.ShapeDtypeStruct((terms, slots, share, size), f32),
            jax.ShapeDtypeStruct(wavefn.shape, f32),
            jax.ShapeDtypeStruct((terms, max(across - wide, 1), size, size), f32),
        ],
        [
            pltpu.SMEM(term_shift.shape, jnp.int32),
            pltpu.VMEM((terms, slots, others, size), f32),
            pltpu.VMEM((terms, wide, size, size), f32),
            *work(others),
            pltpu.SemaphoreType.DMA((5,)),
            pltpu.SemaphoreType.DMA((ny,)),
        ],
    )
    kept.append(keep)
    arrived.append(swap(send))
    send, keep, own = call(
        first_own,
        [lops, psi, right, chosen],
        [VMEM] * 4,
        [result(1, wide)] * 2 + [jax.ShapeDtypeStruct((slots, terms * share, 2 * size), bf16)],
        work(share),
    )
    own_kept.append(keep)
    own_arrived.append(swap(send))
    pieces.append(sums(add_cores, [(blocks(wide), rows, size)] * (ny - 1), [kept[0], arrived[0]], keep))
    for start, wide in zip(starts[1:], widths[1:]):
        *send, keep, right = call(
            functools.partial(later_others, start, widths[0]),
            [left, psi, rops, chosen, pieces[-1][0]],
            [VMEM] * 4 + [ANY],
            [result(ny - 1, 1)] * wide + [
                result(ny - 1, wide), jax.ShapeDtypeStruct((wide, terms, 2 * size, size), bf16)
            ],
            work(others),
        )
        arrived.append([swap(value) for value in send])
        kept.append(keep)
        send, keep = call(
            functools.partial(later_own, start),
            [own, psi, right, chosen, keep],
            [VMEM] * 4 + [ANY],
            [result(1, wide)] * 2,
            work(share),
        )
        own_kept.append(keep)
        own_arrived.append(swap(send))
        pieces.append(sums(
            add_cores, [(blocks(wide), rows, size)] * (ny - 1), [kept[-1], *arrived[-1]], own_kept[-1]
        ))
    arranged = []
    for i, (wide, keep, came) in enumerate(zip(widths, own_kept, own_arrived)):
        landed = [ahead(value, by) for by, value in enumerate(pieces[i], 1)]
        before, after = ([keep, *landed], [came]) if i == 0 else ([keep, came], landed)
        total = sums(add_all, [keep.shape], before, pieces[i + 1][0] if i + 1 < count else None)[0]
        value = sums(add_all, [(slots, wide, rows, size), (second, wide, rows, size)], [total, *after], None, ADD_COST if i == 0 else 1)
        value = [sectors(part, way) for way, part in enumerate(value)]
        value[1] = sums(landed_first, [value[1].shape], [value[1]], None, LANDED_COST)[0]
        if i + 1 < count:
            arranged.append(arrange(slots, *value))
    return settle(arranged, *value)


def solution(mesh):
    placed = (
        P("lsec", "rsec", None, None),
        P("op", "lsec", None, None),
        P("op", "rsec", None, None),
        P("op"),
    )
    return jax.shard_map(
        shards, mesh=mesh, in_specs=placed, out_specs=P("lsec", "rsec", "op", None), check_vma=False
    )
```

profile of v0, /device:TPU:0, one launch (start us, length us, event | category | flops | bytes accessed | tf_op | source)
XLA Modules:
  0.0 30.4 jit_solution(7735929473987544965)
XLA Ops:
  0.0 3.1 %shard_map.46 = (f32[1,14,32,128]{3,2,1,0:T(8,128)S(1)}, f32[1,14,32,128]{3,2,1,0:T(8,128)S(1)}, bf16[4,448,256]{2,1,0:T(8,128)(2,1)S(1)}, bf16[2,7,256,128]{3,2...) custom-call(s32[7]{0:T(128)} %shift.1, ...), custom_call_target="tpu_custom_call" | custom-call | flops 1 | bytes 1024 | tf_op jit(solution)/shard_map/pallas_call | solution.py:156
  3.1 0.5 %collective-permute-start = (f32[1,14,32,128]{3,2,1,0:T(8,128)S(1)}, f32[1,14,32,128]{3,2,1,0:T(8,128)S(1)}, u32[]{:S(2)}, u32[]{:S(2)}) collective-permute-start(f32[1,14,32,128]{3,2,1,0:T(8,128)S(1)} %get-tuple-element.32), channel_id=1, source_target_pairs={{0,8},{1,9},{2,10},{3,11},{4,12},{5,13},{6,14},{7,15},{8,0},{9,1},... | collective-permute-start | bytes 688136 | tf_op jit(solution)/shard_map/ppermute | solution.py:257
  3.6 1.3 %shard_map.47 = (f32[1,14,32,128]{3,2,1,0:T(8,128)S(1)}, f32[1,14,32,128]{3,2,1,0:T(8,128)S(1)}, bf16[4,448,256]{2,1,0:T(8,128)(2,1)S(1)}) custom-call(f32[7,4,64,128]{3,2,1,0:T(8,128)S(1)} %get-tuple-element.26.lops, f32[4,4,128,128]{3,2,1,0:T(8,128)S(1)} %get-tuple-element.27.psi, bf16[2,7,256,128]{3,2,1,0:T(8,128)(2,1)S(1)} %get-tuple-element.28.right, ...), custom_call_target="tpu_custom_call" | custom-call | flops 1 | bytes 1024 | tf_op jit(solution)/shard_map/pallas_call | solution.py:156
  4.9 0.0 collective-permute-done.refs_1_
  5.0 2.7 %collective-permute-start.1 = (f32[14,32,128]{2,1,0:T(8,128)S(1)}, f32[14,32,128]{2,1,0:T(8,128)S(1)}, u32[]{:S(2)}, u32[]{:S(2)}) collective-permute-start(f32[14,32,128]{2,1,0:T(8,128)S(1)} %shard_map.48.after), channel_id=1, source_target_pairs={{0,16},{1,17},{2,18},{3,19},{4,20},{5,21},{6,22},{7,23},{8,24},{9,... | collective-permute-start | bytes 688136 | tf_op jit(solution)/shard_map/ppermute | solution.py:257
  7.7 0.1 collective-permute-start.4
  7.8 1.3 %shard_map.49 = (f32[1,7,32,128]{3,2,1,0:T(8,128)S(1)}, f32[1,7,32,128]{3,2,1,0:T(8,128)S(1)}, f32[1,14,32,128]{3,2,1,0:T(8,128)S(1)}, bf16[2,7,256,128]{3,2,1,0:T(8,128)(2,1)S(1)}) custom-call(bf16[4,448,256]{2,1,0:T(8,128)(2,1)S(1)} %get-tuple-element.33.left, f32[4,4,128,128]{3,2,1,0:T(8,128)S(1)} %get-tuple-element.27.psi, ...), custom_call_target="tpu_custom_call" | custom-call | flops 1 | bytes 1024 | tf_op jit(solution)/shard_map/pallas_call | solution.py:156
  9.1 0.5 %collective-permute-start.2 = (f32[1,7,32,128]{3,2,1,0:T(8,128)S(1)}, f32[1,7,32,128]{3,2,1,0:T(8,128)S(1)}, u32[]{:S(2)}, u32[]{:S(2)}) collective-permute-start(f32[1,7,32,128]{3,2,1,0:T(8,128)S(1)} %get-tuple-element.36), channel_id=1, source_target_pairs={{0,8},{1,9},{2,10},{3,11},{4,12},{5,13},{6,14},{7,15},{8,0},{9,1},... | collective-permute-start | bytes 344072 | tf_op jit(solution)/shard_map/ppermute | solution.py:257
  9.6 0.1 collective-permute-start.3
  9.7 1.3 %shard_map.50 = (f32[1,14,32,128]{3,2,1,0:T(8,128)S(1)}, f32[1,14,32,128]{3,2,1,0:T(8,128)S(1)}) custom-call(bf16[4,448,256]{2,1,0:T(8,128)(2,1)S(1)} %get-tuple-element.38.left, f32[4,4,128,128]{3,2,1,0:T(8,128)S(1)} %get-tuple-element.27.psi, bf16[2,7,256,128]{3,2,1,0:T(8,128)(2,1)S(1)} %get-tuple-element.39.right, ...), custom_call_target="tpu_custom_call" | custom-call | flops 1 | bytes 1024 | tf_op jit(solution)/shard_map/pallas_call | solution.py:156
  11.0 0.5 %collective-permute-start.7 = (f32[1,14,32,128]{3,2,1,0:T(8,128)S(1)}, f32[1,14,32,128]{3,2,1,0:T(8,128)S(1)}, u32[]{:S(2)}, u32[]{:S(2)}) collective-permute-start(f32[1,14,32,128]{3,2,1,0:T(8,128)S(1)} %get-tuple-element.44), channel_id=1, source_target_pairs={{0,8},{1,9},{2,10},{3,11},{4,12},{5,13},{6,14},{7,15},{8,0},{9,1},... | collective-permute-start | bytes 688136 | tf_op jit(solution)/shard_map/ppermute | solution.py:257
  11.5 0.0 collective-permute-done.2.refs_1_
  11.5 0.0 collective-permute-done.3.refs_2_
  11.5 0.1 collective-permute-start.8
  11.7 2.2 %collective-permute-done.1.refs_1_ = f32[14,32,128]{2,1,0:T(8,128)S(1)} collective-permute-done((f32[14,32,128]{2,1,0:T(8,128)S(1)}, f32[14,32,128]{2,1,0:T(8,128)S(1)}, u32[]{:S(2)}, u32[]{:S(2)}) %collective-permute-start.1) | collective-permute-done | bytes 229408 | tf_op jit(solution)/shard_map/ppermute | solution.py:257
  13.9 0.0 collective-permute-done.4.refs_1_
  13.9 2.8 %collective-permute-start.6 = (f32[3,2,32,128]{3,2,1,0:T(8,128)S(1)}, f32[3,2,32,128]{3,2,1,0:T(8,128)S(1)}, u32[]{:S(2)}, u32[]{:S(2)}) collective-permute-start(f32[3,2,32,128]{3,2,1,0:T(8,128)S(1)} %get-tuple-element.43), channel_id=1, source_target_pairs={{0,5},{1,6},{2,7},{3,4},{4,3},{5,0},{6,1},{7,2},{8,13},{9,14},{10,... | collective-permute-start | bytes 294920 | tf_op jit(solution)/shard_map/ppermute | solution.py:257
  16.7 2.5 %collective-permute-start.5 = (f32[4,2,32,128]{3,2,1,0:T(8,128)S(1)}, f32[4,2,32,128]{3,2,1,0:T(8,128)S(1)}, u32[]{:S(2)}, u32[]{:S(2)}) collective-permute-start(f32[4,2,32,128]{3,2,1,0:T(8,128)S(1)} %get-tuple-element.42), channel_id=1, source_target_pairs={{0,7},{1,4},{2,5},{3,6},{4,1},{5,2},{6,3},{7,0},{8,15},{9,12},{10,... | collective-permute-start | bytes 393224 | tf_op jit(solution)/shard_map/ppermute | solution.py:257
  19.2 0.0 collective-permute-done.7.refs_1_
  19.2 0.0 collective-permute-done.8.refs_1_
  19.2 2.5 %collective-permute-start.10 = (f32[3,2,32,128]{3,2,1,0:T(8,128)S(1)}, f32[3,2,32,128]{3,2,1,0:T(8,128)S(1)}, u32[]{:S(2)}, u32[]{:S(2)}) collective-permute-start(f32[3,2,32,128]{3,2,1,0:T(8,128)S(1)} %get-tuple-element.46), channel_id=1, source_target_pairs={{0,5},{1,6},{2,7},{3,4},{4,3},{5,0},{6,1},{7,2},{8,13},{9,14},{10,... | collective-permute-start | bytes 294920 | tf_op jit(solution)/shard_map/ppermute | solution.py:257
  21.8 2.4 %collective-permute-start.9 = (f32[4,2,32,128]{3,2,1,0:T(8,128)S(1)}, f32[4,2,32,128]{3,2,1,0:T(8,128)S(1)}, u32[]{:S(2)}, u32[]{:S(2)}) collective-permute-start(f32[4,2,32,128]{3,2,1,0:T(8,128)S(1)} %get-tuple-element.45), channel_id=1, source_target_pairs={{0,7},{1,4},{2,5},{3,6},{4,1},{5,2},{6,3},{7,0},{8,15},{9,12},{10,... | collective-permute-start | bytes 393224 | tf_op jit(solution)/shard_map/ppermute | solution.py:257
  24.2 0.0 collective-permute-done.6.refs_0_
  24.2 0.8 %collective-permute-done.5.refs_0_ = f32[4,2,32,128]{3,2,1,0:T(8,128)S(1)} collective-permute-done((f32[4,2,32,128]{3,2,1,0:T(8,128)S(1)}, f32[4,2,32,128]{3,2,1,0:T(8,128)S(1)}, u32[]{:S(2)}, u32[]{:S(2)}) %collective-permute-start.5) | collective-permute-done | bytes 131104 | tf_op jit(solution)/shard_map/ppermute | solution.py:257
  25.1 1.9 %collective-permute-done.10.refs_0_ = f32[3,2,32,128]{3,2,1,0:T(8,128)S(1)} collective-permute-done((f32[3,2,32,128]{3,2,1,0:T(8,128)S(1)}, f32[3,2,32,128]{3,2,1,0:T(8,128)S(1)}, u32[]{:S(2)}, u32[]{:S(2)}) %collective-permute-start.10) | collective-permute-done | bytes 98336 | tf_op jit(solution)/shard_map/ppermute | solution.py:257
  27.0 2.6 %collective-permute-done.9.refs_1_ = f32[4,2,32,128]{3,2,1,0:T(8,128)S(1)} collective-permute-done((f32[4,2,32,128]{3,2,1,0:T(8,128)S(1)}, f32[4,2,32,128]{3,2,1,0:T(8,128)S(1)}, u32[]{:S(2)}, u32[]{:S(2)}) %collective-permute-start.9) | collective-permute-done | bytes 131104 | tf_op jit(solution)/shard_map/ppermute | solution.py:257
  29.6 0.8 %shard_map.59 = f32[4,4,32,128]{3,2,1,0:T(8,128)} custom-call(f32[2,4,2,32,128]{4,3,2,1,0:T(8,128)S(1)} %shard_map.55.refs_0_, f32[4,2,32,128]{3,2,1,0:T(8,128)S(1)} %collective-permute-done.9.refs_1_, f32[3,2,32,128]{3,2,1,0:T(8,128)S(1)} %shard_map.58.refs_2_), custom_call_target="tpu_custom_call" | custom-call | flops 1 | bytes 1024 | tf_op jit(solution)/shard_map/pallas_call | solution.py:156
  (9 shorter events, 0.2 us)
Async XLA Ops:
  3.1 1.8 %collective-permute-start = (f32[1,14,32,128]{3,2,1,0:T(8,128)S(1)}, f32[1,14,32,128]{3,2,1,0:T(8,128)S(1)}, u32[]{:S(2)}, u32[]{:S(2)}) collective-permute-start(f32[1,14,32,128]{3,2,1,0:T(8,128)S(1)} %get-tuple-element.32), channel_id=1, source_target_pairs={{0,8},{1,9},{2,10},{3,11},{4,12},{5,13},{6,14},{7,15},{8,0},{9,1},... | collective-permute-start | bytes 688136 | tf_op jit(solution)/shard_map/ppermute | solution.py:257
  5.0 8.9 %collective-permute-start.1 = (f32[14,32,128]{2,1,0:T(8,128)S(1)}, f32[14,32,128]{2,1,0:T(8,128)S(1)}, u32[]{:S(2)}, u32[]{:S(2)}) collective-permute-start(f32[14,32,128]{2,1,0:T(8,128)S(1)} %shard_map.48.after), channel_id=1, source_target_pairs={{0,16},{1,17},{2,18},{3,19},{4,20},{5,21},{6,22},{7,23},{8,24},{9,... | collective-permute-start | bytes 688136 | tf_op jit(solution)/shard_map/ppermute | solution.py:257
  7.7 6.2 %collective-permute-start.4 = (f32[1,14,32,128]{3,2,1,0:T(8,128)S(1)}, f32[1,14,32,128]{3,2,1,0:T(8,128)S(1)}, u32[]{:S(2)}, u32[]{:S(2)}) collective-permute-start(f32[1,14,32,128]{3,2,1,0:T(8,128)S(1)} %get-tuple-element.41), channel_id=1, source_target_pairs={{0,8},{1,9},{2,10},{3,11},{4,12},{5,13},{6,14},{7,15},{8,0},{9,1},... | collective-permute-start | bytes 688136 | tf_op jit(solution)/shard_map/ppermute | solution.py:257
  9.1 2.4 %collective-permute-start.2 = (f32[1,7,32,128]{3,2,1,0:T(8,128)S(1)}, f32[1,7,32,128]{3,2,1,0:T(8,128)S(1)}, u32[]{:S(2)}, u32[]{:S(2)}) collective-permute-start(f32[1,7,32,128]{3,2,1,0:T(8,128)S(1)} %get-tuple-element.36), channel_id=1, source_target_pairs={{0,8},{1,9},{2,10},{3,11},{4,12},{5,13},{6,14},{7,15},{8,0},{9,1},... | collective-permute-start | bytes 344072 | tf_op jit(solution)/shard_map/ppermute | solution.py:257
  9.6 1.9 %collective-permute-start.3 = (f32[1,7,32,128]{3,2,1,0:T(8,128)S(1)}, f32[1,7,32,128]{3,2,1,0:T(8,128)S(1)}, u32[]{:S(2)}, u32[]{:S(2)}) collective-permute-start(f32[1,7,32,128]{3,2,1,0:T(8,128)S(1)} %get-tuple-element.37), channel_id=1, source_target_pairs={{0,8},{1,9},{2,10},{3,11},{4,12},{5,13},{6,14},{7,15},{8,0},{9,1},... | collective-permute-start | bytes 344072 | tf_op jit(solution)/shard_map/ppermute | solution.py:257
  11.0 8.2 %collective-permute-start.7 = (f32[1,14,32,128]{3,2,1,0:T(8,128)S(1)}, f32[1,14,32,128]{3,2,1,0:T(8,128)S(1)}, u32[]{:S(2)}, u32[]{:S(2)}) collective-permute-start(f32[1,14,32,128]{3,2,1,0:T(8,128)S(1)} %get-tuple-element.44), channel_id=1, source_target_pairs={{0,8},{1,9},{2,10},{3,11},{4,12},{5,13},{6,14},{7,15},{8,0},{9,1},... | collective-permute-start | bytes 688136 | tf_op jit(solution)/shard_map/ppermute | solution.py:257
  11.5 7.7 %collective-permute-start.8 = (f32[14,32,128]{2,1,0:T(8,128)S(1)}, f32[14,32,128]{2,1,0:T(8,128)S(1)}, u32[]{:S(2)}, u32[]{:S(2)}) collective-permute-start(f32[14,32,128]{2,1,0:T(8,128)S(1)} %shard_map.51.refs_2_), channel_id=1, source_target_pairs={{0,16},{1,17},{2,18},{3,19},{4,20},{5,21},{6,22},{7,23},{8,24},{9,... | collective-permute-start | bytes 688136 | tf_op jit(solution)/shard_map/ppermute | solution.py:257
  13.9 10.3 %collective-permute-start.6 = (f32[3,2,32,128]{3,2,1,0:T(8,128)S(1)}, f32[3,2,32,128]{3,2,1,0:T(8,128)S(1)}, u32[]{:S(2)}, u32[]{:S(2)}) collective-permute-start(f32[3,2,32,128]{3,2,1,0:T(8,128)S(1)} %get-tuple-element.43), channel_id=1, source_target_pairs={{0,5},{1,6},{2,7},{3,4},{4,3},{5,0},{6,1},{7,2},{8,13},{9,14},{10,... | collective-permute-start | bytes 294920 | tf_op jit(solution)/shard_map/ppermute | solution.py:257
  16.7 8.4 %collective-permute-start.5 = (f32[4,2,32,128]{3,2,1,0:T(8,128)S(1)}, f32[4,2,32,128]{3,2,1,0:T(8,128)S(1)}, u32[]{:S(2)}, u32[]{:S(2)}) collective-permute-start(f32[4,2,32,128]{3,2,1,0:T(8,128)S(1)} %get-tuple-element.42), channel_id=1, source_target_pairs={{0,7},{1,4},{2,5},{3,6},{4,1},{5,2},{6,3},{7,0},{8,15},{9,12},{10,... | collective-permute-start | bytes 393224 | tf_op jit(solution)/shard_map/ppermute | solution.py:257
  19.2 7.8 %collective-permute-start.10 = (f32[3,2,32,128]{3,2,1,0:T(8,128)S(1)}, f32[3,2,32,128]{3,2,1,0:T(8,128)S(1)}, u32[]{:S(2)}, u32[]{:S(2)}) collective-permute-start(f32[3,2,32,128]{3,2,1,0:T(8,128)S(1)} %get-tuple-element.46), channel_id=1, source_target_pairs={{0,5},{1,6},{2,7},{3,4},{4,3},{5,0},{6,1},{7,2},{8,13},{9,14},{10,... | collective-permute-start | bytes 294920 | tf_op jit(solution)/shard_map/ppermute | solution.py:257
  21.8 7.8 %collective-permute-start.9 = (f32[4,2,32,128]{3,2,1,0:T(8,128)S(1)}, f32[4,2,32,128]{3,2,1,0:T(8,128)S(1)}, u32[]{:S(2)}, u32[]{:S(2)}) collective-permute-start(f32[4,2,32,128]{3,2,1,0:T(8,128)S(1)} %get-tuple-element.45), channel_id=1, source_target_pairs={{0,7},{1,4},{2,5},{3,6},{4,1},{5,2},{6,3},{7,0},{8,15},{9,12},{10,... | collective-permute-start | bytes 393224 | tf_op jit(solution)/shard_map/ppermute | solution.py:257
where the time goes:
time: 30.6 us; the launch traced here: 30.4 us
  starting transfers between devices  14.8 us (48%)
  Pallas kernels  7.98 us (26%)
  waiting for transfers between devices  7.53 us (25%)
    ppermute x11, starting transfers between devices, permute(): return lax.ppermute(value, ('op', 'lsec', 'rsec'), perm)  14.8 us
    pallas_call x14, Pallas kernels, call(): pl.pallas_call(kernel, in_specs=in_specs, out_specs=[VMEM] * len(out_shap...  7.98 us
    ppermute x11, waiting for transfers between devices, permute(): return lax.ppermute(value, ('op', 'lsec', 'rsec'), perm)  7.53 us
  transfers between devices with their start and end apart: 11, of which 4 were waited for; matrix products, arithmetic and copies ran while one was open for 0% of the time, Pallas kernels for 13%

commit v1 on v0

--- a/solution.py
+++ b/solution.py
@@ -7,7 +7,6 @@
 from jax.experimental.pallas import tpu as pltpu
 from jax.sharding import PartitionSpec as P
 
-WIDTHS = (2, 2)
 CORES = 2
 ARRANGE_COST = 1
 ADD_COST = 2 * 10 ** 9
@@ -287,8 +286,9 @@
                 out[...] = refs[0][at] + refs[1][at]
             else:
                 wide = len(refs) - 1
-                for block in range(out.shape[0]):
-                    out[block] = refs[0][at, block] + refs[1 + block % wide][at, block // wide]
+                first = 0 if at % 2 else slots * wide
+                for block in range(first, first + out.shape[0]):
+                    out[block - first] = refs[0][at // 2, block] + refs[1 + block % wide][at // 2, block // wide]
 
     def add_all(refs, outs):
         total = refs[0][...]
@@ -306,9 +306,8 @@
     def landed_first(refs, outs):
         outs[0][...] = refs[0][...]
 
-    widths = WIDTHS if sum(WIDTHS) == across else (across,)
+    widths = (across // 2, across - across // 2)
     starts = [sum(widths[:i]) for i in range(len(widths))]
-    count = len(widths)
     pieces, own_kept, own_arrived, arrived, kept = [], [], [], [], []
 
     arguments = (term_shift, wavefn, left_ops, right_ops)
@@ -367,20 +366,38 @@
         )
         own_kept.append(keep)
         own_arrived.append(swap(send))
-        pieces.append(sums(
-            add_cores, [(blocks(wide), rows, size)] * (ny - 1), [kept[-1], *arrived[-1]], own_kept[-1]
-        ))
-    arranged = []
-    for i, (wide, keep, came) in enumerate(zip(widths, own_kept, own_arrived)):
-        landed = [ahead(value, by) for by, value in enumerate(pieces[i], 1)]
-        before, after = ([keep, *landed], [came]) if i == 0 else ([keep, came], landed)
-        total = sums(add_all, [keep.shape], before, pieces[i + 1][0] if i + 1 < count else None)[0]
-        value = sums(add_all, [(slots, wide, rows, size), (second, wide, rows, size)], [total, *after], None, ADD_COST if i == 0 else 1)
-        value = [sectors(part, way) for way, part in enumerate(value)]
-        value[1] = sums(landed_first, [value[1].shape], [value[1]], None, LANDED_COST)[0]
-        if i + 1 < count:
-            arranged.append(arrange(slots, *value))
-    return settle(arranged, *value)
+        groups = [(number * wide, rows, size) for number in (second, slots)]
+        pieces.append(sums(add_cores, groups * (ny - 1), [kept[-1], *arrived[-1]], own_kept[-1]))
+
+    def land(values):
+        return [ahead(value, by) for by, value in enumerate(values, 1)]
+
+    wide = widths[0]
+    total = sums(add_all, [own_kept[0].shape], [own_kept[0], *land(pieces[0])], pieces[1][0])[0]
+    value = sums(
+        add_all, [(slots, wide, rows, size), (second, wide, rows, size)], [total, own_arrived[0]], None, ADD_COST
+    )
+    ready = value[1]
+    value = [sectors(part, way) for way, part in enumerate(value)]
+    value[1] = sums(landed_first, [value[1].shape], [value[1]], None, LANDED_COST)[0]
+    arranged = [arrange(slots, *value)]
+
+    wide = widths[1]
+    total = sums(add_all, [(blocks(wide), rows, size)], [own_kept[1], own_arrived[1]], ready)[0]
+
+    def add_group(refs, outs):
+        block = refs[0][first:first + refs[1].shape[0]]
+        for ref in refs[1:]:
+            block = block + ref[...]
+        outs[0][...] = block.reshape(outs[0].shape)
+
+    value = []
+    for way, number, first in ((1, second, slots * wide), (0, slots, 0)):
+        came = land(pieces[1][1 - way::2])
+        ready = sums(add_group, [(number, wide, rows, size)], [total, *came], ready)[0]
+        value.append(sectors(ready, way))
+    value[0] = sums(landed_first, [value[0].shape], [value[0]], arranged[0], LANDED_COST)[0]
+    return settle(arranged, value[1], value[0])
 
 
 def solution(mesh):

time: 30.6 us -> 30.4 us (level)
  waiting for transfers between devices: 7.53 us -> 5.86 us
  starting transfers between devices: 14.8 us -> 16.3 us
    ppermute x11 -> x12, waiting for transfers between devices: 7.53 us -> 5.86 us  [permute(): return lax.ppermute(value, ('op', 'lsec', 'rsec'), perm)]
    ppermute x11 -> x12, starting transfers between devices: 14.8 us -> 16.3 us  [permute(): return lax.ppermute(value, ('op', 'lsec', 'rsec'), perm)]
    pallas_call x14 -> x15, Pallas kernels: 7.98 us -> 7.98 us  [call(): pl.pallas_call(kernel, in_specs=in_specs, out_specs=[VMEM] * len(out_shap...]
  transfers between devices with their start and end apart: 11 -> 12, of which waited for: 4 -> 4; matrix products, arithmetic and copies ran while one was open for 0% -> 0% of each run, Pallas kernels for 13% -> 14%
where the time goes in v1:
time: 30.4 us; the launch traced here: 30.2 us
  starting transfers between devices  16.3 us (54%)
  Pallas kernels  7.98 us (26%)
  waiting for transfers between devices  5.86 us (19%)
    ppermute x12, starting transfers between devices, permute(): return lax.ppermute(value, ('op', 'lsec', 'rsec'), perm)  16.3 us
    pallas_call x15, Pallas kernels, call(): pl.pallas_call(kernel, in_specs=in_specs, out_specs=[VMEM] * len(out_shap...  7.98 us
    ppermute x12, waiting for transfers between devices, permute(): return lax.ppermute(value, ('op', 'lsec', 'rsec'), perm)  5.86 us
  transfers between devices with their start and end apart: 12, of which 4 were waited for; matrix products, arithmetic and copies ran while one was open for 0% of the time, Pallas kernels for 14%

profile of v1, /device:TPU:0, one launch (start us, length us, event | category | flops | bytes accessed | tf_op | source)
XLA Modules:
  0.0 30.2 jit_solution(14975707507305344375)
XLA Ops:
  0.0 3.1 %shard_map.46 = (f32[1,14,32,128]{3,2,1,0:T(8,128)S(1)}, f32[1,14,32,128]{3,2,1,0:T(8,128)S(1)}, bf16[4,448,256]{2,1,0:T(8,128)(2,1)S(1)}, bf16[2,7,256,128]{3,2...) custom-call(s32[7]{0:T(128)} %shift.1, ...), custom_call_target="tpu_custom_call" | custom-call | flops 1 | bytes 1024 | tf_op jit(solution)/shard_map/pallas_call | solution.py:155
  3.1 0.5 %collective-permute-start = (f32[1,14,32,128]{3,2,1,0:T(8,128)S(1)}, f32[1,14,32,128]{3,2,1,0:T(8,128)S(1)}, u32[]{:S(2)}, u32[]{:S(2)}) collective-permute-start(f32[1,14,32,128]{3,2,1,0:T(8,128)S(1)} %get-tuple-element.32), channel_id=1, source_target_pairs={{0,8},{1,9},{2,10},{3,11},{4,12},{5,13},{6,14},{7,15},{8,0},{9,1},... | collective-permute-start | bytes 688136 | tf_op jit(solution)/shard_map/ppermute | solution.py:256
  3.6 1.3 %shard_map.47 = (f32[1,14,32,128]{3,2,1,0:T(8,128)S(1)}, f32[1,14,32,128]{3,2,1,0:T(8,128)S(1)}, bf16[4,448,256]{2,1,0:T(8,128)(2,1)S(1)}) custom-call(f32[7,4,64,128]{3,2,1,0:T(8,128)S(1)} %get-tuple-element.26.lops, f32[4,4,128,128]{3,2,1,0:T(8,128)S(1)} %get-tuple-element.27.psi, bf16[2,7,256,128]{3,2,1,0:T(8,128)(2,1)S(1)} %get-tuple-element.28.right, ...), custom_call_target="tpu_custom_call" | custom-call | flops 1 | bytes 1024 | tf_op jit(solution)/shard_map/pallas_call | solution.py:155
  4.9 0.0 collective-permute-done.refs_1_
  5.0 2.7 %collective-permute-start.1 = (f32[14,32,128]{2,1,0:T(8,128)S(1)}, f32[14,32,128]{2,1,0:T(8,128)S(1)}, u32[]{:S(2)}, u32[]{:S(2)}) collective-permute-start(f32[14,32,128]{2,1,0:T(8,128)S(1)} %shard_map.48.after), channel_id=1, source_target_pairs={{0,16},{1,17},{2,18},{3,19},{4,20},{5,21},{6,22},{7,23},{8,24},{9,... | collective-permute-start | bytes 688136 | tf_op jit(solution)/shard_map/ppermute | solution.py:256
  7.7 0.1 collective-permute-start.4
  7.8 1.3 %shard_map.49 = (f32[1,7,32,128]{3,2,1,0:T(8,128)S(1)}, f32[1,7,32,128]{3,2,1,0:T(8,128)S(1)}, f32[1,14,32,128]{3,2,1,0:T(8,128)S(1)}, bf16[2,7,256,128]{3,2,1,0:T(8,128)(2,1)S(1)}) custom-call(bf16[4,448,256]{2,1,0:T(8,128)(2,1)S(1)} %get-tuple-element.33.left, f32[4,4,128,128]{3,2,1,0:T(8,128)S(1)} %get-tuple-element.27.psi, ...), custom_call_target="tpu_custom_call" | custom-call | flops 1 | bytes 1024 | tf_op jit(solution)/shard_map/pallas_call | solution.py:155
  9.1 0.5 %collective-permute-start.2 = (f32[1,7,32,128]{3,2,1,0:T(8,128)S(1)}, f32[1,7,32,128]{3,2,1,0:T(8,128)S(1)}, u32[]{:S(2)}, u32[]{:S(2)}) collective-permute-start(f32[1,7,32,128]{3,2,1,0:T(8,128)S(1)} %get-tuple-element.36), channel_id=1, source_target_pairs={{0,8},{1,9},{2,10},{3,11},{4,12},{5,13},{6,14},{7,15},{8,0},{9,1},... | collective-permute-start | bytes 344072 | tf_op jit(solution)/shard_map/ppermute | solution.py:256
  9.6 0.1 collective-permute-start.3
  9.7 1.3 %shard_map.50 = (f32[1,14,32,128]{3,2,1,0:T(8,128)S(1)}, f32[1,14,32,128]{3,2,1,0:T(8,128)S(1)}) custom-call(bf16[4,448,256]{2,1,0:T(8,128)(2,1)S(1)} %get-tuple-element.38.left, f32[4,4,128,128]{3,2,1,0:T(8,128)S(1)} %get-tuple-element.27.psi, bf16[2,7,256,128]{3,2,1,0:T(8,128)(2,1)S(1)} %get-tuple-element.39.right, ...), custom_call_target="tpu_custom_call" | custom-call | flops 1 | bytes 1024 | tf_op jit(solution)/shard_map/pallas_call | solution.py:155
  11.0 0.5 %collective-permute-start.7 = (f32[1,14,32,128]{3,2,1,0:T(8,128)S(1)}, f32[1,14,32,128]{3,2,1,0:T(8,128)S(1)}, u32[]{:S(2)}, u32[]{:S(2)}) collective-permute-start(f32[1,14,32,128]{3,2,1,0:T(8,128)S(1)} %get-tuple-element.45), channel_id=1, source_target_pairs={{0,8},{1,9},{2,10},{3,11},{4,12},{5,13},{6,14},{7,15},{8,0},{9,1},... | collective-permute-start | bytes 688136 | tf_op jit(solution)/shard_map/ppermute | solution.py:256
  11.5 0.0 collective-permute-done.2.refs_1_
  11.5 0.0 collective-permute-done.3.refs_2_
  11.5 0.1 collective-permute-start.9
  11.7 1.9 %collective-permute-start.8 = (f32[8,32,128]{2,1,0:T(8,128)S(1)}, f32[8,32,128]{2,1,0:T(8,128)S(1)}, u32[]{:S(2)}, u32[]{:S(2)}) collective-permute-start(f32[8,32,128]{2,1,0:T(8,128)S(1)} %get-tuple-element.46), channel_id=1, source_target_pairs={{0,16},{1,17},{2,18},{3,19},{4,20},{5,21},{6,22},{7,23},{8,24},{9,... | collective-permute-start | bytes 393224 | tf_op jit(solution)/shard_map/ppermute | solution.py:256
  13.6 0.2 collective-permute-done.1.refs_1_
  13.9 0.0 collective-permute-done.4.refs_1_
  13.9 2.8 %collective-permute-start.6 = (f32[3,2,32,128]{3,2,1,0:T(8,128)S(1)}, f32[3,2,32,128]{3,2,1,0:T(8,128)S(1)}, u32[]{:S(2)}, u32[]{:S(2)}) collective-permute-start(f32[3,2,32,128]{3,2,1,0:T(8,128)S(1)} %get-tuple-element.44.refs_2_), channel_id=1, source_target_pairs={{0,5},{1,6},{2,7},{3,4},{4,3},{5,0},{6,1},{7,2},{8,13},{9,14},{10,... | collective-permute-start | bytes 294920 | tf_op jit(solution)/shard_map/ppermute | solution.py:256
  16.7 2.5 %collective-permute-start.5 = (f32[4,2,32,128]{3,2,1,0:T(8,128)S(1)}, f32[4,2,32,128]{3,2,1,0:T(8,128)S(1)}, u32[]{:S(2)}, u32[]{:S(2)}) collective-permute-start(f32[4,2,32,128]{3,2,1,0:T(8,128)S(1)} %get-tuple-element.43), channel_id=1, source_target_pairs={{0,7},{1,4},{2,5},{3,6},{4,1},{5,2},{6,3},{7,0},{8,15},{9,12},{10,... | collective-permute-start | bytes 393224 | tf_op jit(solution)/shard_map/ppermute | solution.py:256
  19.2 0.0 collective-permute-done.7.refs_1_
  19.2 0.0 collective-permute-done.9.refs_1_
  19.2 1.7 %collective-permute-start.11 = (f32[3,2,32,128]{3,2,1,0:T(8,128)S(1)}, f32[3,2,32,128]{3,2,1,0:T(8,128)S(1)}, u32[]{:S(2)}, u32[]{:S(2)}) collective-permute-start(f32[3,2,32,128]{3,2,1,0:T(8,128)S(1)} %shard_map.57.refs_2_), channel_id=1, source_target_pairs={{0,5},{1,6},{2,7},{3,4},{4,3},{5,0},{6,1},{7,2},{8,13},{9,14},{10,... | collective-permute-start | bytes 294920 | tf_op jit(solution)/shard_map/ppermute | solution.py:256
  20.9 0.0 collective-permute-done.8.refs_1_
  20.9 2.9 %collective-permute-start.10 = (f32[4,2,32,128]{3,2,1,0:T(8,128)S(1)}, f32[4,2,32,128]{3,2,1,0:T(8,128)S(1)}, u32[]{:S(2)}, u32[]{:S(2)}) collective-permute-start(f32[4,2,32,128]{3,2,1,0:T(8,128)S(1)} %shard_map.58), channel_id=1, source_target_pairs={{0,7},{1,4},{2,5},{3,6},{4,1},{5,2},{6,3},{7,0},{8,15},{9,12},{10,... | collective-permute-start | bytes 393224 | tf_op jit(solution)/shard_map/ppermute | solution.py:256
  23.8 0.0 collective-permute-done.6.refs_0_
  23.8 2.0 %collective-permute-done.5.refs_0_ = f32[4,2,32,128]{3,2,1,0:T(8,128)S(1)} collective-permute-done((f32[4,2,32,128]{3,2,1,0:T(8,128)S(1)}, f32[4,2,32,128]{3,2,1,0:T(8,128)S(1)}, u32[]{:S(2)}, u32[]{:S(2)}) %collective-permute-start.5) | collective-permute-done | bytes 131104 | tf_op jit(solution)/shard_map/ppermute | solution.py:256
  25.9 1.6 %collective-permute-done.11.refs_0_ = f32[3,2,32,128]{3,2,1,0:T(8,128)S(1)} collective-permute-done((f32[3,2,32,128]{3,2,1,0:T(8,128)S(1)}, f32[3,2,32,128]{3,2,1,0:T(8,128)S(1)}, u32[]{:S(2)}, u32[]{:S(2)}) %collective-permute-start.11) | collective-permute-done | bytes 98336 | tf_op jit(solution)/shard_map/ppermute | solution.py:256
  27.4 2.1 %collective-permute-done.10.refs_1_ = f32[4,2,32,128]{3,2,1,0:T(8,128)S(1)} collective-permute-done((f32[4,2,32,128]{3,2,1,0:T(8,128)S(1)}, f32[4,2,32,128]{3,2,1,0:T(8,128)S(1)}, u32[]{:S(2)}, u32[]{:S(2)}) %collective-permute-start.10) | collective-permute-done | bytes 131104 | tf_op jit(solution)/shard_map/ppermute | solution.py:256
  29.5 0.8 %shard_map.60 = f32[4,4,32,128]{3,2,1,0:T(8,128)} custom-call(f32[2,4,2,32,128]{4,3,2,1,0:T(8,128)S(1)} %shard_map.55.refs_1_.refs_0_, f32[4,2,32,128]{3,2,1,0:T(8,128)S(1)} %collective-permute-done.10.refs_1_, f32[3,2,32,128]{3,2,1,0:T(8,128)S(1)} %shard_map.59.refs_2_), custom_call_target="tpu_custom_call" | custom-call | flops 1 | bytes 1024 | tf_op jit(solution)/shard_map/pallas_call | solution.py:155
  (10 shorter events, 0.2 us)
Async XLA Ops:
  3.1 1.8 %collective-permute-start = (f32[1,14,32,128]{3,2,1,0:T(8,128)S(1)}, f32[1,14,32,128]{3,2,1,0:T(8,128)S(1)}, u32[]{:S(2)}, u32[]{:S(2)}) collective-permute-start(f32[1,14,32,128]{3,2,1,0:T(8,128)S(1)} %get-tuple-element.32), channel_id=1, source_target_pairs={{0,8},{1,9},{2,10},{3,11},{4,12},{5,13},{6,14},{7,15},{8,0},{9,1},... | collective-permute-start | bytes 688136 | tf_op jit(solution)/shard_map/ppermute | solution.py:256
  5.0 8.9 %collective-permute-start.1 = (f32[14,32,128]{2,1,0:T(8,128)S(1)}, f32[14,32,128]{2,1,0:T(8,128)S(1)}, u32[]{:S(2)}, u32[]{:S(2)}) collective-permute-start(f32[14,32,128]{2,1,0:T(8,128)S(1)} %shard_map.48.after), channel_id=1, source_target_pairs={{0,16},{1,17},{2,18},{3,19},{4,20},{5,21},{6,22},{7,23},{8,24},{9,... | collective-permute-start | bytes 688136 | tf_op jit(solution)/shard_map/ppermute | solution.py:256
  7.7 6.2 %collective-permute-start.4 = (f32[1,14,32,128]{3,2,1,0:T(8,128)S(1)}, f32[1,14,32,128]{3,2,1,0:T(8,128)S(1)}, u32[]{:S(2)}, u32[]{:S(2)}) collective-permute-start(f32[1,14,32,128]{3,2,1,0:T(8,128)S(1)} %get-tuple-element.42), channel_id=1, source_target_pairs={{0,8},{1,9},{2,10},{3,11},{4,12},{5,13},{6,14},{7,15},{8,0},{9,1},... | collective-permute-start | bytes 688136 | tf_op jit(solution)/shard_map/ppermute | solution.py:256
  9.1 2.4 %collective-permute-start.2 = (f32[1,7,32,128]{3,2,1,0:T(8,128)S(1)}, f32[1,7,32,128]{3,2,1,0:T(8,128)S(1)}, u32[]{:S(2)}, u32[]{:S(2)}) collective-permute-start(f32[1,7,32,128]{3,2,1,0:T(8,128)S(1)} %get-tuple-element.36), channel_id=1, source_target_pairs={{0,8},{1,9},{2,10},{3,11},{4,12},{5,13},{6,14},{7,15},{8,0},{9,1},... | collective-permute-start | bytes 344072 | tf_op jit(solution)/shard_map/ppermute | solution.py:256
  9.6 1.9 %collective-permute-start.3 = (f32[1,7,32,128]{3,2,1,0:T(8,128)S(1)}, f32[1,7,32,128]{3,2,1,0:T(8,128)S(1)}, u32[]{:S(2)}, u32[]{:S(2)}) collective-permute-start(f32[1,7,32,128]{3,2,1,0:T(8,128)S(1)} %get-tuple-element.37), channel_id=1, source_target_pairs={{0,8},{1,9},{2,10},{3,11},{4,12},{5,13},{6,14},{7,15},{8,0},{9,1},... | collective-permute-start | bytes 344072 | tf_op jit(solution)/shard_map/ppermute | solution.py:256
  11.0 8.2 %collective-permute-start.7 = (f32[1,14,32,128]{3,2,1,0:T(8,128)S(1)}, f32[1,14,32,128]{3,2,1,0:T(8,128)S(1)}, u32[]{:S(2)}, u32[]{:S(2)}) collective-permute-start(f32[1,14,32,128]{3,2,1,0:T(8,128)S(1)} %get-tuple-element.45), channel_id=1, source_target_pairs={{0,8},{1,9},{2,10},{3,11},{4,12},{5,13},{6,14},{7,15},{8,0},{9,1},... | collective-permute-start | bytes 688136 | tf_op jit(solution)/shard_map/ppermute | solution.py:256
  11.5 7.7 %collective-permute-start.9 = (f32[6,32,128]{2,1,0:T(8,128)S(1)}, f32[6,32,128]{2,1,0:T(8,128)S(1)}, u32[]{:S(2)}, u32[]{:S(2)}) collective-permute-start(f32[6,32,128]{2,1,0:T(8,128)S(1)} %get-tuple-element.41.refs_2_), channel_id=1, source_target_pairs={{0,16},{1,17},{2,18},{3,19},{4,20},{5,21},{6,22},{7,23},{8,24},{9,... | collective-permute-start | bytes 294920 | tf_op jit(solution)/shard_map/ppermute | solution.py:256
  11.7 9.2 %collective-permute-start.8 = (f32[8,32,128]{2,1,0:T(8,128)S(1)}, f32[8,32,128]{2,1,0:T(8,128)S(1)}, u32[]{:S(2)}, u32[]{:S(2)}) collective-permute-start(f32[8,32,128]{2,1,0:T(8,128)S(1)} %get-tuple-element.46), channel_id=1, source_target_pairs={{0,16},{1,17},{2,18},{3,19},{4,20},{5,21},{6,22},{7,23},{8,24},{9,... | collective-permute-start | bytes 393224 | tf_op jit(solution)/shard_map/ppermute | solution.py:256
  13.9 9.9 %collective-permute-start.6 = (f32[3,2,32,128]{3,2,1,0:T(8,128)S(1)}, f32[3,2,32,128]{3,2,1,0:T(8,128)S(1)}, u32[]{:S(2)}, u32[]{:S(2)}) collective-permute-start(f32[3,2,32,128]{3,2,1,0:T(8,128)S(1)} %get-tuple-element.44.refs_2_), channel_id=1, source_target_pairs={{0,5},{1,6},{2,7},{3,4},{4,3},{5,0},{6,1},{7,2},{8,13},{9,14},{10,... | collective-permute-start | bytes 294920 | tf_op jit(solution)/shard_map/ppermute | solution.py:256
  16.7 9.1 %collective-permute-start.5 = (f32[4,2,32,128]{3,2,1,0:T(8,128)S(1)}, f32[4,2,32,128]{3,2,1,0:T(8,128)S(1)}, u32[]{:S(2)}, u32[]{:S(2)}) collective-permute-start(f32[4,2,32,128]{3,2,1,0:T(8,128)S(1)} %get-tuple-element.43), channel_id=1, source_target_pairs={{0,7},{1,4},{2,5},{3,6},{4,1},{5,2},{6,3},{7,0},{8,15},{9,12},{10,... | collective-permute-start | bytes 393224 | tf_op jit(solution)/shard_map/ppermute | solution.py:256
  19.2 8.2 %collective-permute-start.11 = (f32[3,2,32,128]{3,2,1,0:T(8,128)S(1)}, f32[3,2,32,128]{3,2,1,0:T(8,128)S(1)}, u32[]{:S(2)}, u32[]{:S(2)}) collective-permute-start(f32[3,2,32,128]{3,2,1,0:T(8,128)S(1)} %shard_map.57.refs_2_), channel_id=1, source_target_pairs={{0,5},{1,6},{2,7},{3,4},{4,3},{5,0},{6,1},{7,2},{8,13},{9,14},{10,... | collective-permute-start | bytes 294920 | tf_op jit(solution)/shard_map/ppermute | solution.py:256
  20.9 8.6 %collective-permute-start.10 = (f32[4,2,32,128]{3,2,1,0:T(8,128)S(1)}, f32[4,2,32,128]{3,2,1,0:T(8,128)S(1)}, u32[]{:S(2)}, u32[]{:S(2)}) collective-permute-start(f32[4,2,32,128]{3,2,1,0:T(8,128)S(1)} %shard_map.58), channel_id=1, source_target_pairs={{0,7},{1,4},{2,5},{3,6},{4,1},{5,2},{6,3},{7,0},{8,15},{9,12},{10,... | collective-permute-start | bytes 393224 | tf_op jit(solution)/shard_map/ppermute | solution.py:256

commit v2 on v1

--- a/solution.py
+++ b/solution.py
@@ -36,7 +36,7 @@
     return core * (rows // 8), (1 - core) * (rows // 8), skipped(slots, second) * (many // 8)
 
 
-def products(left, psi, right, chosen, inner, total, send, keep, start, begins, lops=None, rops=None, ready=()):
+def products(left, psi, right, way_of, inner, total, send, keep, start, begins, lops=None, rops=None, ready=()):
     slots, height, twice = left.shape
     size = twice // 2
     wide, terms = right.shape[:2]
@@ -57,6 +57,7 @@
         if r == 0:
             for copy in ready:
                 copy.wait()
+        total[...] = jnp.zeros_like(total)
         for t in range(terms):
             if rops is not None:
                 right[r, t] = jnp.concatenate(split(rops[t, r]), axis=0)
@@ -65,9 +66,8 @@
                 inner[t], jnp.concatenate([both, both], axis=1), NT, preferred_element_type=jnp.float32
             )
             out = (out[:, :size] + out[:, size:]).reshape(-1, 8, size)
-            for way in range(2):
-                mine = out * chosen[t, way]
-                total[way] = mine if t == 0 else total[way] + mine
+            way = way_of(t)
+            total[way] = total[way] + out
         for chip in range(chips):
             for at in range(slots + second):
                 way = 0 if at < slots else 1
@@ -85,7 +85,7 @@
     return 0 if second == slots else 1 - lax.axis_index("lsec")
 
 
-def first_others(shift, psi, lops, rops, send, keep, left, right, chosen, lops_own, psi_all, rops_rest, *refs):
+def first_others(shift, psi, lops, rops, send, keep, left, right, lops_own, psi_all, rops_rest, *refs):
     bits, lops_now, rops_now, inner, total, sems, lsems = refs
     terms, slots, size, _ = lops.shape
     wide = right.shape[0]
@@ -112,17 +112,13 @@
         copy.start()
     second = keep.shape[1] // wide - slots
     begins = lines(lops_now.shape[2], keep.shape[2], slots, second)
-    flip = lax.axis_index("lsec") if second < slots else 0
+    way_of = classes(bits, second < slots)
     for copy in copies:
         copy.wait()
     for copy in later:
         copy.start()
-    for t in range(terms):
-        kept = jnp.where(flip == 1, 1 - bits[t], bits[t]).astype(jnp.float32)
-        chosen[t, 0] = jnp.full((8, size), kept, jnp.float32)
-        chosen[t, 1] = jnp.full((8, size), 1.0 - kept, jnp.float32)
     products(
-        left, psi_all, right, chosen, inner, total, send, keep, 0, begins, lops_now, rops_now, ready
+        left, psi_all, right, way_of, inner, total, send, keep, 0, begins, lops_now, rops_now, ready
     )
     for copy in later:
         copy.wait()
@@ -134,21 +130,33 @@
     return lines(height // terms, keep.shape[2], slots, keep.shape[1] // wide - slots)
 
 
-def first_own(lops, psi, right, chosen, send, keep, left, inner, total):
-    products(left, psi, right, chosen, inner, total, send, keep, 0, find(left, keep, right), lops)
-
-
-def later_others(start, skip, left, psi, rops, chosen, after, *refs):
-    wide = refs[-3].shape[0]
-    send, (keep, right, inner, total) = refs[:wide], refs[wide:]
+def classes(bits, paired):
+    flip = lax.axis_index("lsec") if paired else 0
+    return lambda t: jnp.where(flip == 1, bits[t], 1 - bits[t])
+
+
+def again(shift, left, psi, right, inner, total, bits, sem, send, keep, start, **extra):
+    copy = pltpu.make_async_copy(shift, bits, sem.at[0])
+    copy.start()
+    paired = keep.shape[1] < 2 * right.shape[0] * left.shape[0]
     products(
-        left, psi, right, chosen, inner, total, send, keep, start, find(left, keep, right),
-        rops=rops.at[:, start - skip:],
-    )
-
-
-def later_own(start, left, psi, right, chosen, after, send, keep, inner, total):
-    products(left, psi, right, chosen, inner, total, send, keep, start, find(left, keep, right))
+        left, psi, right, classes(bits, paired), inner, total, send, keep, start, find(left, keep, right),
+        ready=[copy], **extra,
+    )
+
+
+def first_own(shift, lops, psi, right, send, keep, left, inner, total, bits, sem):
+    again(shift, left, psi, right, inner, total, bits, sem, send, keep, 0, lops=lops)
+
+
+def later_others(start, skip, shift, left, psi, rops, after, *refs):
+    wide = refs[-5].shape[0]
+    send, (keep, right, inner, total, bits, sem) = refs[:wide], refs[wide:]
+    again(shift, left, psi, right, inner, total, bits, sem, send, keep, start, rops=rops.at[:, start - skip:])
+
+
+def later_own(start, shift, left, psi, right, after, send, keep, inner, total, bits, sem):
+    again(shift, left, psi, right, inner, total, bits, sem, send, keep, start)
 
 
 def call(kernel, operands, in_specs, out_shape, scratch=(), flops=1):
@@ -310,16 +318,19 @@
     starts = [sum(widths[:i]) for i in range(len(widths))]
     pieces, own_kept, own_arrived, arrived, kept = [], [], [], [], []
 
-    arguments = (term_shift, wavefn, left_ops, right_ops)
+    fetch = [pltpu.SMEM(term_shift.shape, jnp.int32), pltpu.SemaphoreType.DMA((1,))]
+    arguments = [
+        pltpu.with_memory_space_constraint(value, pltpu.HBM)
+        for value in (term_shift, wavefn, left_ops, right_ops)
+    ]
     wide = widths[0]
-    send, keep, left, right, chosen, lops, psi, rops = call(
+    send, keep, left, right, lops, psi, rops = call(
         first_others,
-        [pltpu.with_memory_space_constraint(value, pltpu.HBM) for value in arguments],
+        arguments,
         [HBM] * 4,
         [result(ny - 1, wide)] * 2 + [
             jax.ShapeDtypeStruct((slots, terms * others, 2 * size), bf16),
             jax.ShapeDtypeStruct((wide, terms, 2 * size, size), bf16),
-            jax.ShapeDtypeStruct((terms, 2, 8, size), f32),
             jax.ShapeDtypeStruct((terms, slots, share, size), f32),
             jax.ShapeDtypeStruct(wavefn.shape, f32),
             jax.ShapeDtypeStruct((terms, max(across - wide, 1), size, size), f32),
@@ -337,10 +348,10 @@
     arrived.append(swap(send))
     send, keep, own = call(
         first_own,
-        [lops, psi, right, chosen],
-        [VMEM] * 4,
+        [arguments[0], lops, psi, right],
+        [HBM] + [VMEM] * 3,
         [result(1, wide)] * 2 + [jax.ShapeDtypeStruct((slots, terms * share, 2 * size), bf16)],
-        work(share),
+        work(share) + fetch,
     )
     own_kept.append(keep)
     own_arrived.append(swap(send))
@@ -348,21 +359,21 @@
     for start, wide in zip(starts[1:], widths[1:]):
         *send, keep, right = call(
             functools.partial(later_others, start, widths[0]),
-            [left, psi, rops, chosen, pieces[-1][0]],
-            [VMEM] * 4 + [ANY],
+            [arguments[0], left, psi, rops, pieces[-1][0]],
+            [HBM] + [VMEM] * 3 + [ANY],
             [result(ny - 1, 1)] * wide + [
                 result(ny - 1, wide), jax.ShapeDtypeStruct((wide, terms, 2 * size, size), bf16)
             ],
-            work(others),
+            work(others) + fetch,
         )
         arrived.append([swap(value) for value in send])
         kept.append(keep)
         send, keep = call(
             functools.partial(later_own, start),
-            [own, psi, right, chosen, keep],
-            [VMEM] * 4 + [ANY],
+            [arguments[0], own, psi, right, keep],
+            [HBM] + [VMEM] * 3 + [ANY],
             [result(1, wide)] * 2,
-            work(share),
+            work(share) + fetch,
         )
         own_kept.append(keep)
         own_arrived.append(swap(send))
@@ -379,7 +390,6 @@
     )
     ready = value[1]
     value = [sectors(part, way) for way, part in enumerate(value)]
-    value[1] = sums(landed_first, [value[1].shape], [value[1]], None, LANDED_COST)[0]
     arranged = [arrange(slots, *value)]
 
     wide = widths[1]

time: 30.4 us -> 31.1 us (1.023)
  Pallas kernels: 7.98 us -> 9.13 us
  waiting for transfers between devices: 5.86 us -> 5.15 us
    pallas_call x15 -> x14, Pallas kernels: 7.98 us -> 9.13 us  [call(): pl.pallas_call(kernel, in_specs=in_specs, out_specs=[VMEM] * len(out_shap...]
    ppermute x12, waiting for transfers between devices: 5.86 us -> 5.15 us  [permute(): return lax.ppermute(value, ('op', 'lsec', 'rsec'), perm)]
  transfers between devices with their start and end apart: 12 -> 12, of which waited for: 4 -> 3; matrix products, arithmetic and copies ran while one was open for 0% -> 0% of each run, Pallas kernels for 14% -> 17%
where the time goes in v2:
time: 31.1 us; the launch traced here: 30.9 us
  starting transfers between devices  16.5 us (53%)
  Pallas kernels  9.13 us (29%)
  waiting for transfers between devices  5.15 us (17%)
    ppermute x12, starting transfers between devices, permute(): return lax.ppermute(value, ('op', 'lsec', 'rsec'), perm)  16.5 us
    pallas_call x14, Pallas kernels, call(): pl.pallas_call(kernel, in_specs=in_specs, out_specs=[VMEM] * len(out_shap...  9.13 us
    ppermute x12, waiting for transfers between devices, permute(): return lax.ppermute(value, ('op', 'lsec', 'rsec'), perm)  5.15 us
  transfers between devices with their start and end apart: 12, of which 3 were waited for; matrix products, arithmetic and copies ran while one was open for 0% of the time, Pallas kernels for 17%

profile of v2, /device:TPU:0, one launch (start us, length us, event | category | flops | bytes accessed | tf_op | source)
XLA Modules:
  0.0 30.9 jit_solution(13804206856578884445)
XLA Ops:
  0.0 3.1 %shard_map.46 = (f32[1,14,32,128]{3,2,1,0:T(8,128)S(1)}, f32[1,14,32,128]{3,2,1,0:T(8,128)S(1)}, bf16[4,448,256]{2,1,0:T(8,128)(2,1)S(1)}, bf16[2,7,256,128]{3,2...) custom-call(s32[7]{0:T(128)} %shift.7, ...), custom_call_target="tpu_custom_call" | custom-call | flops 1 | bytes 1024 | tf_op jit(solution)/shard_map/pallas_call | solution.py:163
  3.1 0.5 %collective-permute-start = (f32[1,14,32,128]{3,2,1,0:T(8,128)S(1)}, f32[1,14,32,128]{3,2,1,0:T(8,128)S(1)}, u32[]{:S(2)}, u32[]{:S(2)}) collective-permute-start(f32[1,14,32,128]{3,2,1,0:T(8,128)S(1)} %get-tuple-element.30), channel_id=1, source_target_pairs={{0,8},{1,9},{2,10},{3,11},{4,12},{5,13},{6,14},{7,15},{8,0},{9,1},... | collective-permute-start | bytes 688136 | tf_op jit(solution)/shard_map/ppermute | solution.py:264
  3.6 1.7 %shard_map.47 = (f32[1,14,32,128]{3,2,1,0:T(8,128)S(1)}, f32[1,14,32,128]{3,2,1,0:T(8,128)S(1)}, bf16[4,448,256]{2,1,0:T(8,128)(2,1)S(1)}) custom-call(s32[7]{0:T(128)} %shift.7, f32[7,4,64,128]{3,2,1,0:T(8,128)S(1)} %get-tuple-element.25.lops, f32[4,4,128,128]{3,2,1,0:T(8,128)S(1)} %get-tuple-element.26.psi, ...), custom_call_target="tpu_custom_call" | custom-call | flops 1 | bytes 1024 | tf_op jit(solution)/shard_map/pallas_call | solution.py:163
  5.3 0.0 collective-permute-done.refs_1_
  5.4 2.6 %collective-permute-start.1 = (f32[14,32,128]{2,1,0:T(8,128)S(1)}, f32[14,32,128]{2,1,0:T(8,128)S(1)}, u32[]{:S(2)}, u32[]{:S(2)}) collective-permute-start(f32[14,32,128]{2,1,0:T(8,128)S(1)} %shard_map.48.after), channel_id=1, source_target_pairs={{0,16},{1,17},{2,18},{3,19},{4,20},{5,21},{6,22},{7,23},{8,24},{9,... | collective-permute-start | bytes 688136 | tf_op jit(solution)/shard_map/ppermute | solution.py:264
  8.0 0.2 collective-permute-start.4
  8.2 1.7 %shard_map.49 = (f32[1,7,32,128]{3,2,1,0:T(8,128)S(1)}, f32[1,7,32,128]{3,2,1,0:T(8,128)S(1)}, f32[1,14,32,128]{3,2,1,0:T(8,128)S(1)}, bf16[2,7,256,128]{3,2,1,0:T(8,128)(2,1)S(1)}) custom-call(s32[7]{0:T(128)} %shift.7, bf16[4,448,256]{2,1,0:T(8,128)(2,1)S(1)} %get-tuple-element.31.left, f32[4,4,128,128]{3,2,1,0:T(8,128)S(1)} %get-tuple-element.26.psi, ...), custom_call_target="tpu_custom_call" | custom-call | flops 1 | bytes 1024 | tf_op jit(solution)/shard_map/pallas_call | solution.py:163
  9.9 0.4 %collective-permute-start.2 = (f32[1,7,32,128]{3,2,1,0:T(8,128)S(1)}, f32[1,7,32,128]{3,2,1,0:T(8,128)S(1)}, u32[]{:S(2)}, u32[]{:S(2)}) collective-permute-start(f32[1,7,32,128]{3,2,1,0:T(8,128)S(1)} %get-tuple-element.34), channel_id=1, source_target_pairs={{0,8},{1,9},{2,10},{3,11},{4,12},{5,13},{6,14},{7,15},{8,0},{9,1},... | collective-permute-start | bytes 344072 | tf_op jit(solution)/shard_map/ppermute | solution.py:264
  10.3 0.2 collective-permute-start.3
  10.5 1.7 %shard_map.50 = (f32[1,14,32,128]{3,2,1,0:T(8,128)S(1)}, f32[1,14,32,128]{3,2,1,0:T(8,128)S(1)}) custom-call(s32[7]{0:T(128)} %shift.7, bf16[4,448,256]{2,1,0:T(8,128)(2,1)S(1)} %get-tuple-element.36.left, f32[4,4,128,128]{3,2,1,0:T(8,128)S(1)} %get-tuple-element.26.psi, bf16[2,7,256,128]{3,2,1,0:T(8,128)(2,1)S(1)} %get-tuple-element.37.right, ...), custom_call_target="tpu_custom_call" | custom-call | flops 1 | bytes 1024 | tf_op jit(solution)/shard_map/pallas_call | solution.py:163
  12.2 0.4 %collective-permute-start.7 = (f32[1,14,32,128]{3,2,1,0:T(8,128)S(1)}, f32[1,14,32,128]{3,2,1,0:T(8,128)S(1)}, u32[]{:S(2)}, u32[]{:S(2)}) collective-permute-start(f32[1,14,32,128]{3,2,1,0:T(8,128)S(1)} %get-tuple-element.43), channel_id=1, source_target_pairs={{0,8},{1,9},{2,10},{3,11},{4,12},{5,13},{6,14},{7,15},{8,0},{9,1},... | collective-permute-start | bytes 688136 | tf_op jit(solution)/shard_map/ppermute | solution.py:264
  12.5 0.0 collective-permute-done.2.refs_1_
  12.5 0.0 collective-permute-done.3.refs_2_
  12.6 0.2 collective-permute-start.9
  12.8 1.9 %collective-permute-start.8 = (f32[8,32,128]{2,1,0:T(8,128)S(1)}, f32[8,32,128]{2,1,0:T(8,128)S(1)}, u32[]{:S(2)}, u32[]{:S(2)}) collective-permute-start(f32[8,32,128]{2,1,0:T(8,128)S(1)} %get-tuple-element.44), channel_id=1, source_target_pairs={{0,16},{1,17},{2,18},{3,19},{4,20},{5,21},{6,22},{7,23},{8,24},{9,... | collective-permute-start | bytes 393224 | tf_op jit(solution)/shard_map/ppermute | solution.py:264
  14.6 0.0 collective-permute-done.1.refs_1_
  14.7 0.0 collective-permute-done.4.refs_1_
  14.7 4.6 %collective-permute-start.5 = (f32[4,2,32,128]{3,2,1,0:T(8,128)S(1)}, f32[4,2,32,128]{3,2,1,0:T(8,128)S(1)}, u32[]{:S(2)}, u32[]{:S(2)}) collective-permute-start(f32[4,2,32,128]{3,2,1,0:T(8,128)S(1)} %get-tuple-element.41), channel_id=1, source_target_pairs={{0,7},{1,4},{2,5},{3,6},{4,1},{5,2},{6,3},{7,0},{8,15},{9,12},{10,... | collective-permute-start | bytes 393224 | tf_op jit(solution)/shard_map/ppermute | solution.py:264
  19.3 0.0 collective-permute-start.6
  19.3 0.0 collective-permute-done.7.refs_1_
  19.4 0.0 collective-permute-done.9.refs_1_
  19.4 3.0 %collective-permute-start.11 = (f32[3,2,32,128]{3,2,1,0:T(8,128)S(1)}, f32[3,2,32,128]{3,2,1,0:T(8,128)S(1)}, u32[]{:S(2)}, u32[]{:S(2)}) collective-permute-start(f32[3,2,32,128]{3,2,1,0:T(8,128)S(1)} %shard_map.56.refs_2_), channel_id=1, source_target_pairs={{0,5},{1,6},{2,7},{3,4},{4,3},{5,0},{6,1},{7,2},{8,13},{9,14},{10,... | collective-permute-start | bytes 294920 | tf_op jit(solution)/shard_map/ppermute | solution.py:264
  22.4 0.0 collective-permute-done.8.refs_1_
  22.4 2.6 %collective-permute-start.10 = (f32[4,2,32,128]{3,2,1,0:T(8,128)S(1)}, f32[4,2,32,128]{3,2,1,0:T(8,128)S(1)}, u32[]{:S(2)}, u32[]{:S(2)}) collective-permute-start(f32[4,2,32,128]{3,2,1,0:T(8,128)S(1)} %shard_map.57), channel_id=1, source_target_pairs={{0,7},{1,4},{2,5},{3,6},{4,1},{5,2},{6,3},{7,0},{8,15},{9,12},{10,... | collective-permute-start | bytes 393224 | tf_op jit(solution)/shard_map/ppermute | solution.py:264
  25.0 1.0 %collective-permute-done.6.refs_1_ = f32[3,2,32,128]{3,2,1,0:T(8,128)S(1)} collective-permute-done((f32[3,2,32,128]{3,2,1,0:T(8,128)S(1)}, f32[3,2,32,128]{3,2,1,0:T(8,128)S(1)}, u32[]{:S(2)}, u32[]{:S(2)}) %collective-permute-start.6) | collective-permute-done | bytes 98336 | tf_op jit(solution)/shard_map/ppermute | solution.py:264
  26.0 0.0 collective-permute-done.5.refs_0_
  26.0 2.6 %collective-permute-done.11.refs_0_ = f32[3,2,32,128]{3,2,1,0:T(8,128)S(1)} collective-permute-done((f32[3,2,32,128]{3,2,1,0:T(8,128)S(1)}, f32[3,2,32,128]{3,2,1,0:T(8,128)S(1)}, u32[]{:S(2)}, u32[]{:S(2)}) %collective-permute-start.11) | collective-permute-done | bytes 98336 | tf_op jit(solution)/shard_map/ppermute | solution.py:264
  28.7 1.5 %collective-permute-done.10.refs_1_ = f32[4,2,32,128]{3,2,1,0:T(8,128)S(1)} collective-permute-done((f32[4,2,32,128]{3,2,1,0:T(8,128)S(1)}, f32[4,2,32,128]{3,2,1,0:T(8,128)S(1)}, u32[]{:S(2)}, u32[]{:S(2)}) %collective-permute-start.10) | collective-permute-done | bytes 131104 | tf_op jit(solution)/shard_map/ppermute | solution.py:264
  30.1 0.8 %shard_map.59 = f32[4,4,32,128]{3,2,1,0:T(8,128)} custom-call(f32[2,4,2,32,128]{4,3,2,1,0:T(8,128)S(1)} %shard_map.54.refs_1_.refs_0_, f32[4,2,32,128]{3,2,1,0:T(8,128)S(1)} %collective-permute-done.10.refs_1_, f32[3,2,32,128]{3,2,1,0:T(8,128)S(1)} %shard_map.58.refs_2_), custom_call_target="tpu_custom_call" | custom-call | flops 1 | bytes 1024 | tf_op jit(solution)/shard_map/pallas_call | solution.py:163
  (9 shorter events, 0.2 us)
Async XLA Ops:
  3.1 2.2 %collective-permute-start = (f32[1,14,32,128]{3,2,1,0:T(8,128)S(1)}, f32[1,14,32,128]{3,2,1,0:T(8,128)S(1)}, u32[]{:S(2)}, u32[]{:S(2)}) collective-permute-start(f32[1,14,32,128]{3,2,1,0:T(8,128)S(1)} %get-tuple-element.30), channel_id=1, source_target_pairs={{0,8},{1,9},{2,10},{3,11},{4,12},{5,13},{6,14},{7,15},{8,0},{9,1},... | collective-permute-start | bytes 688136 | tf_op jit(solution)/shard_map/ppermute | solution.py:264
  5.4 9.3 %collective-permute-start.1 = (f32[14,32,128]{2,1,0:T(8,128)S(1)}, f32[14,32,128]{2,1,0:T(8,128)S(1)}, u32[]{:S(2)}, u32[]{:S(2)}) collective-permute-start(f32[14,32,128]{2,1,0:T(8,128)S(1)} %shard_map.48.after), channel_id=1, source_target_pairs={{0,16},{1,17},{2,18},{3,19},{4,20},{5,21},{6,22},{7,23},{8,24},{9,... | collective-permute-start | bytes 688136 | tf_op jit(solution)/shard_map/ppermute | solution.py:264
  8.0 6.7 %collective-permute-start.4 = (f32[1,14,32,128]{3,2,1,0:T(8,128)S(1)}, f32[1,14,32,128]{3,2,1,0:T(8,128)S(1)}, u32[]{:S(2)}, u32[]{:S(2)}) collective-permute-start(f32[1,14,32,128]{3,2,1,0:T(8,128)S(1)} %get-tuple-element.40), channel_id=1, source_target_pairs={{0,8},{1,9},{2,10},{3,11},{4,12},{5,13},{6,14},{7,15},{8,0},{9,1},... | collective-permute-start | bytes 688136 | tf_op jit(solution)/shard_map/ppermute | solution.py:264
  9.9 2.6 %collective-permute-start.2 = (f32[1,7,32,128]{3,2,1,0:T(8,128)S(1)}, f32[1,7,32,128]{3,2,1,0:T(8,128)S(1)}, u32[]{:S(2)}, u32[]{:S(2)}) collective-permute-start(f32[1,7,32,128]{3,2,1,0:T(8,128)S(1)} %get-tuple-element.34), channel_id=1, source_target_pairs={{0,8},{1,9},{2,10},{3,11},{4,12},{5,13},{6,14},{7,15},{8,0},{9,1},... | collective-permute-start | bytes 344072 | tf_op jit(solution)/shard_map/ppermute | solution.py:264
  10.3 2.3 %collective-permute-start.3 = (f32[1,7,32,128]{3,2,1,0:T(8,128)S(1)}, f32[1,7,32,128]{3,2,1,0:T(8,128)S(1)}, u32[]{:S(2)}, u32[]{:S(2)}) collective-permute-start(f32[1,7,32,128]{3,2,1,0:T(8,128)S(1)} %get-tuple-element.35), channel_id=1, source_target_pairs={{0,8},{1,9},{2,10},{3,11},{4,12},{5,13},{6,14},{7,15},{8,0},{9,1},... | collective-permute-start | bytes 344072 | tf_op jit(solution)/shard_map/ppermute | solution.py:264
  12.2 7.2 %collective-permute-start.7 = (f32[1,14,32,128]{3,2,1,0:T(8,128)S(1)}, f32[1,14,32,128]{3,2,1,0:T(8,128)S(1)}, u32[]{:S(2)}, u32[]{:S(2)}) collective-permute-start(f32[1,14,32,128]{3,2,1,0:T(8,128)S(1)} %get-tuple-element.43), channel_id=1, source_target_pairs={{0,8},{1,9},{2,10},{3,11},{4,12},{5,13},{6,14},{7,15},{8,0},{9,1},... | collective-permute-start | bytes 688136 | tf_op jit(solution)/shard_map/ppermute | solution.py:264
  12.6 6.8 %collective-permute-start.9 = (f32[6,32,128]{2,1,0:T(8,128)S(1)}, f32[6,32,128]{2,1,0:T(8,128)S(1)}, u32[]{:S(2)}, u32[]{:S(2)}) collective-permute-start(f32[6,32,128]{2,1,0:T(8,128)S(1)} %get-tuple-element.39.refs_2_), channel_id=1, source_target_pairs={{0,16},{1,17},{2,18},{3,19},{4,20},{5,21},{6,22},{7,23},{8,24},{9,... | collective-permute-start | bytes 294920 | tf_op jit(solution)/shard_map/ppermute | solution.py:264
  12.8 9.6 %collective-permute-start.8 = (f32[8,32,128]{2,1,0:T(8,128)S(1)}, f32[8,32,128]{2,1,0:T(8,128)S(1)}, u32[]{:S(2)}, u32[]{:S(2)}) collective-permute-start(f32[8,32,128]{2,1,0:T(8,128)S(1)} %get-tuple-element.44), channel_id=1, source_target_pairs={{0,16},{1,17},{2,18},{3,19},{4,20},{5,21},{6,22},{7,23},{8,24},{9,... | collective-permute-start | bytes 393224 | tf_op jit(solution)/shard_map/ppermute | solution.py:264
  14.7 11.3 %collective-permute-start.5 = (f32[4,2,32,128]{3,2,1,0:T(8,128)S(1)}, f32[4,2,32,128]{3,2,1,0:T(8,128)S(1)}, u32[]{:S(2)}, u32[]{:S(2)}) collective-permute-start(f32[4,2,32,128]{3,2,1,0:T(8,128)S(1)} %get-tuple-element.41), channel_id=1, source_target_pairs={{0,7},{1,4},{2,5},{3,6},{4,1},{5,2},{6,3},{7,0},{8,15},{9,12},{10,... | collective-permute-start | bytes 393224 | tf_op jit(solution)/shard_map/ppermute | solution.py:264
  19.3 6.7 %collective-permute-start.6 = (f32[3,2,32,128]{3,2,1,0:T(8,128)S(1)}, f32[3,2,32,128]{3,2,1,0:T(8,128)S(1)}, u32[]{:S(2)}, u32[]{:S(2)}) collective-permute-start(f32[3,2,32,128]{3,2,1,0:T(8,128)S(1)} %get-tuple-element.42.refs_2_), channel_id=1, source_target_pairs={{0,5},{1,6},{2,7},{3,4},{4,3},{5,0},{6,1},{7,2},{8,13},{9,14},{10,... | collective-permute-start | bytes 294920 | tf_op jit(solution)/shard_map/ppermute | solution.py:264
  19.4 9.3 %collective-permute-start.11 = (f32[3,2,32,128]{3,2,1,0:T(8,128)S(1)}, f32[3,2,32,128]{3,2,1,0:T(8,128)S(1)}, u32[]{:S(2)}, u32[]{:S(2)}) collective-permute-start(f32[3,2,32,128]{3,2,1,0:T(8,128)S(1)} %shard_map.56.refs_2_), channel_id=1, source_target_pairs={{0,5},{1,6},{2,7},{3,4},{4,3},{5,0},{6,1},{7,2},{8,13},{9,14},{10,... | collective-permute-start | bytes 294920 | tf_op jit(solution)/shard_map/ppermute | solution.py:264
  22.4 7.7 %collective-permute-start.10 = (f32[4,2,32,128]{3,2,1,0:T(8,128)S(1)}, f32[4,2,32,128]{3,2,1,0:T(8,128)S(1)}, u32[]{:S(2)}, u32[]{:S(2)}) collective-permute-start(f32[4,2,32,128]{3,2,1,0:T(8,128)S(1)} %shard_map.57), channel_id=1, source_target_pairs={{0,7},{1,4},{2,5},{3,6},{4,1},{5,2},{6,3},{7,0},{8,15},{9,12},{10,... | collective-permute-start | bytes 393224 | tf_op jit(solution)/shard_map/ppermute | solution.py:264

commit v3 on v1

--- a/solution.py
+++ b/solution.py
@@ -65,16 +65,19 @@
                 inner[t], jnp.concatenate([both, both], axis=1), NT, preferred_element_type=jnp.float32
             )
             out = (out[:, :size] + out[:, size:]).reshape(-1, 8, size)
-            for way in range(2):
-                mine = out * chosen[t, way]
-                total[way] = mine if t == 0 else total[way] + mine
+            mine = out * chosen[t, 0]
+            total[0] = mine if t == 0 else total[0] + mine
+            total[1] = out if t == 0 else total[1] + out
         for chip in range(chips):
             for at in range(slots + second):
                 way = 0 if at < slots else 1
                 l = at if at < slots else at - slots
                 for ref, begin in ((keep, here), (send, there)):
                     line = begin + (l * many + chip * CORES * rows) // 8 + (skip if way else 0)
-                    block = total[way, pl.ds(line, rows // 8)].reshape(rows, size)
+                    block = total[way, pl.ds(line, rows // 8)]
+                    if way:
+                        block = block - total[0, pl.ds(line, rows // 8)]
+                    block = block.reshape(rows, size)
                     if isinstance(ref, (list, tuple)):
                         ref[r][chip, at] = block
                     else:

time: 30.4 us -> 30.4 us (level)
  no operation moved by 1% of the time
where the time goes in v3:
time: 30.4 us; the launch traced here: 30.3 us
  starting transfers between devices  16.3 us (54%)
  Pallas kernels  8.05 us (26%)
  waiting for transfers between devices  5.77 us (19%)
    ppermute x12, starting transfers between devices, permute(): return lax.ppermute(value, ('op', 'lsec', 'rsec'), perm)  16.3 us
    pallas_call x15, Pallas kernels, call(): pl.pallas_call(kernel, in_specs=in_specs, out_specs=[VMEM] * len(out_shap...  8.05 us
    ppermute x12, waiting for transfers between devices, permute(): return lax.ppermute(value, ('op', 'lsec', 'rsec'), perm)  5.77 us
  transfers between devices with their start and end apart: 12, of which 4 were waited for; matrix products, arithmetic and copies ran while one was open for 0% of the time, Pallas kernels for 14%

profile of v3, /device:TPU:0, one launch (start us, length us, event | category | flops | bytes accessed | tf_op | source)
XLA Modules:
  0.0 30.3 jit_solution(11641732630265682692)
XLA Ops:
  0.0 3.1 %shard_map.46 = (f32[1,14,32,128]{3,2,1,0:T(8,128)S(1)}, f32[1,14,32,128]{3,2,1,0:T(8,128)S(1)}, bf16[4,448,256]{2,1,0:T(8,128)(2,1)S(1)}, bf16[2,7,256,128]{3,2...) custom-call(s32[7]{0:T(128)} %shift.1, ...), custom_call_target="tpu_custom_call" | custom-call | flops 1 | bytes 1024 | tf_op jit(solution)/shard_map/pallas_call | solution.py:158
  3.1 0.5 %collective-permute-start = (f32[1,14,32,128]{3,2,1,0:T(8,128)S(1)}, f32[1,14,32,128]{3,2,1,0:T(8,128)S(1)}, u32[]{:S(2)}, u32[]{:S(2)}) collective-permute-start(f32[1,14,32,128]{3,2,1,0:T(8,128)S(1)} %get-tuple-element.32), channel_id=1, source_target_pairs={{0,8},{1,9},{2,10},{3,11},{4,12},{5,13},{6,14},{7,15},{8,0},{9,1},... | collective-permute-start | bytes 688136 | tf_op jit(solution)/shard_map/ppermute | solution.py:259
  3.6 1.3 %shard_map.47 = (f32[1,14,32,128]{3,2,1,0:T(8,128)S(1)}, f32[1,14,32,128]{3,2,1,0:T(8,128)S(1)}, bf16[4,448,256]{2,1,0:T(8,128)(2,1)S(1)}) custom-call(f32[7,4,64,128]{3,2,1,0:T(8,128)S(1)} %get-tuple-element.26.lops, f32[4,4,128,128]{3,2,1,0:T(8,128)S(1)} %get-tuple-element.27.psi, bf16[2,7,256,128]{3,2,1,0:T(8,128)(2,1)S(1)} %get-tuple-element.28.right, ...), custom_call_target="tpu_custom_call" | custom-call | flops 1 | bytes 1024 | tf_op jit(solution)/shard_map/pallas_call | solution.py:158
  4.9 0.0 collective-permute-done.refs_1_
  5.0 2.7 %collective-permute-start.1 = (f32[14,32,128]{2,1,0:T(8,128)S(1)}, f32[14,32,128]{2,1,0:T(8,128)S(1)}, u32[]{:S(2)}, u32[]{:S(2)}) collective-permute-start(f32[14,32,128]{2,1,0:T(8,128)S(1)} %shard_map.48.after), channel_id=1, source_target_pairs={{0,16},{1,17},{2,18},{3,19},{4,20},{5,21},{6,22},{7,23},{8,24},{9,... | collective-permute-start | bytes 688136 | tf_op jit(solution)/shard_map/ppermute | solution.py:259
  7.7 0.1 collective-permute-start.4
  7.8 1.4 %shard_map.49 = (f32[1,7,32,128]{3,2,1,0:T(8,128)S(1)}, f32[1,7,32,128]{3,2,1,0:T(8,128)S(1)}, f32[1,14,32,128]{3,2,1,0:T(8,128)S(1)}, bf16[2,7,256,128]{3,2,1,0:T(8,128)(2,1)S(1)}) custom-call(bf16[4,448,256]{2,1,0:T(8,128)(2,1)S(1)} %get-tuple-element.33.left, f32[4,4,128,128]{3,2,1,0:T(8,128)S(1)} %get-tuple-element.27.psi, ...), custom_call_target="tpu_custom_call" | custom-call | flops 1 | bytes 1024 | tf_op jit(solution)/shard_map/pallas_call | solution.py:158
  9.2 0.5 %collective-permute-start.2 = (f32[1,7,32,128]{3,2,1,0:T(8,128)S(1)}, f32[1,7,32,128]{3,2,1,0:T(8,128)S(1)}, u32[]{:S(2)}, u32[]{:S(2)}) collective-permute-start(f32[1,7,32,128]{3,2,1,0:T(8,128)S(1)} %get-tuple-element.36), channel_id=1, source_target_pairs={{0,8},{1,9},{2,10},{3,11},{4,12},{5,13},{6,14},{7,15},{8,0},{9,1},... | collective-permute-start | bytes 344072 | tf_op jit(solution)/shard_map/ppermute | solution.py:259
  9.7 0.1 collective-permute-start.3
  9.7 1.3 %shard_map.50 = (f32[1,14,32,128]{3,2,1,0:T(8,128)S(1)}, f32[1,14,32,128]{3,2,1,0:T(8,128)S(1)}) custom-call(bf16[4,448,256]{2,1,0:T(8,128)(2,1)S(1)} %get-tuple-element.38.left, f32[4,4,128,128]{3,2,1,0:T(8,128)S(1)} %get-tuple-element.27.psi, bf16[2,7,256,128]{3,2,1,0:T(8,128)(2,1)S(1)} %get-tuple-element.39.right, ...), custom_call_target="tpu_custom_call" | custom-call | flops 1 | bytes 1024 | tf_op jit(solution)/shard_map/pallas_call | solution.py:158
  11.0 0.5 %collective-permute-start.7 = (f32[1,14,32,128]{3,2,1,0:T(8,128)S(1)}, f32[1,14,32,128]{3,2,1,0:T(8,128)S(1)}, u32[]{:S(2)}, u32[]{:S(2)}) collective-permute-start(f32[1,14,32,128]{3,2,1,0:T(8,128)S(1)} %get-tuple-element.45), channel_id=1, source_target_pairs={{0,8},{1,9},{2,10},{3,11},{4,12},{5,13},{6,14},{7,15},{8,0},{9,1},... | collective-permute-start | bytes 688136 | tf_op jit(solution)/shard_map/ppermute | solution.py:259
  11.6 0.0 collective-permute-done.2.refs_1_
  11.6 0.0 collective-permute-done.3.refs_2_
  11.6 0.1 collective-permute-start.9
  11.7 1.9 %collective-permute-start.8 = (f32[8,32,128]{2,1,0:T(8,128)S(1)}, f32[8,32,128]{2,1,0:T(8,128)S(1)}, u32[]{:S(2)}, u32[]{:S(2)}) collective-permute-start(f32[8,32,128]{2,1,0:T(8,128)S(1)} %get-tuple-element.46), channel_id=1, source_target_pairs={{0,16},{1,17},{2,18},{3,19},{4,20},{5,21},{6,22},{7,23},{8,24},{9,... | collective-permute-start | bytes 393224 | tf_op jit(solution)/shard_map/ppermute | solution.py:259
  13.7 0.2 collective-permute-done.1.refs_1_
  13.9 0.0 collective-permute-done.4.refs_1_
  13.9 2.8 %collective-permute-start.6 = (f32[3,2,32,128]{3,2,1,0:T(8,128)S(1)}, f32[3,2,32,128]{3,2,1,0:T(8,128)S(1)}, u32[]{:S(2)}, u32[]{:S(2)}) collective-permute-start(f32[3,2,32,128]{3,2,1,0:T(8,128)S(1)} %get-tuple-element.44.refs_2_), channel_id=1, source_target_pairs={{0,5},{1,6},{2,7},{3,4},{4,3},{5,0},{6,1},{7,2},{8,13},{9,14},{10,... | collective-permute-start | bytes 294920 | tf_op jit(solution)/shard_map/ppermute | solution.py:259
  16.7 2.5 %collective-permute-start.5 = (f32[4,2,32,128]{3,2,1,0:T(8,128)S(1)}, f32[4,2,32,128]{3,2,1,0:T(8,128)S(1)}, u32[]{:S(2)}, u32[]{:S(2)}) collective-permute-start(f32[4,2,32,128]{3,2,1,0:T(8,128)S(1)} %get-tuple-element.43), channel_id=1, source_target_pairs={{0,7},{1,4},{2,5},{3,6},{4,1},{5,2},{6,3},{7,0},{8,15},{9,12},{10,... | collective-permute-start | bytes 393224 | tf_op jit(solution)/shard_map/ppermute | solution.py:259
  19.2 0.0 collective-permute-done.7.refs_1_
  19.2 0.0 collective-permute-done.9.refs_1_
  19.2 1.7 %collective-permute-start.11 = (f32[3,2,32,128]{3,2,1,0:T(8,128)S(1)}, f32[3,2,32,128]{3,2,1,0:T(8,128)S(1)}, u32[]{:S(2)}, u32[]{:S(2)}) collective-permute-start(f32[3,2,32,128]{3,2,1,0:T(8,128)S(1)} %shard_map.57.refs_2_), channel_id=1, source_target_pairs={{0,5},{1,6},{2,7},{3,4},{4,3},{5,0},{6,1},{7,2},{8,13},{9,14},{10,... | collective-permute-start | bytes 294920 | tf_op jit(solution)/shard_map/ppermute | solution.py:259
  20.9 0.0 collective-permute-done.8.refs_1_
  20.9 2.9 %collective-permute-start.10 = (f32[4,2,32,128]{3,2,1,0:T(8,128)S(1)}, f32[4,2,32,128]{3,2,1,0:T(8,128)S(1)}, u32[]{:S(2)}, u32[]{:S(2)}) collective-permute-start(f32[4,2,32,128]{3,2,1,0:T(8,128)S(1)} %shard_map.58), channel_id=1, source_target_pairs={{0,7},{1,4},{2,5},{3,6},{4,1},{5,2},{6,3},{7,0},{8,15},{9,12},{10,... | collective-permute-start | bytes 393224 | tf_op jit(solution)/shard_map/ppermute | solution.py:259
  23.9 0.0 collective-permute-done.6.refs_0_
  23.9 2.0 %collective-permute-done.5.refs_0_ = f32[4,2,32,128]{3,2,1,0:T(8,128)S(1)} collective-permute-done((f32[4,2,32,128]{3,2,1,0:T(8,128)S(1)}, f32[4,2,32,128]{3,2,1,0:T(8,128)S(1)}, u32[]{:S(2)}, u32[]{:S(2)}) %collective-permute-start.5) | collective-permute-done | bytes 131104 | tf_op jit(solution)/shard_map/ppermute | solution.py:259
  25.9 1.6 %collective-permute-done.11.refs_0_ = f32[3,2,32,128]{3,2,1,0:T(8,128)S(1)} collective-permute-done((f32[3,2,32,128]{3,2,1,0:T(8,128)S(1)}, f32[3,2,32,128]{3,2,1,0:T(8,128)S(1)}, u32[]{:S(2)}, u32[]{:S(2)}) %collective-permute-start.11) | collective-permute-done | bytes 98336 | tf_op jit(solution)/shard_map/ppermute | solution.py:259
  27.5 2.0 %collective-permute-done.10.refs_1_ = f32[4,2,32,128]{3,2,1,0:T(8,128)S(1)} collective-permute-done((f32[4,2,32,128]{3,2,1,0:T(8,128)S(1)}, f32[4,2,32,128]{3,2,1,0:T(8,128)S(1)}, u32[]{:S(2)}, u32[]{:S(2)}) %collective-permute-start.10) | collective-permute-done | bytes 131104 | tf_op jit(solution)/shard_map/ppermute | solution.py:259
  29.5 0.8 %shard_map.60 = f32[4,4,32,128]{3,2,1,0:T(8,128)} custom-call(f32[2,4,2,32,128]{4,3,2,1,0:T(8,128)S(1)} %shard_map.55.refs_1_.refs_0_, f32[4,2,32,128]{3,2,1,0:T(8,128)S(1)} %collective-permute-done.10.refs_1_, f32[3,2,32,128]{3,2,1,0:T(8,128)S(1)} %shard_map.59.refs_2_), custom_call_target="tpu_custom_call" | custom-call | flops 1 | bytes 1024 | tf_op jit(solution)/shard_map/pallas_call | solution.py:158
  (10 shorter events, 0.2 us)
Async XLA Ops:
  3.1 1.9 %collective-permute-start = (f32[1,14,32,128]{3,2,1,0:T(8,128)S(1)}, f32[1,14,32,128]{3,2,1,0:T(8,128)S(1)}, u32[]{:S(2)}, u32[]{:S(2)}) collective-permute-start(f32[1,14,32,128]{3,2,1,0:T(8,128)S(1)} %get-tuple-element.32), channel_id=1, source_target_pairs={{0,8},{1,9},{2,10},{3,11},{4,12},{5,13},{6,14},{7,15},{8,0},{9,1},... | collective-permute-start | bytes 688136 | tf_op jit(solution)/shard_map/ppermute | solution.py:259
  5.0 8.9 %collective-permute-start.1 = (f32[14,32,128]{2,1,0:T(8,128)S(1)}, f32[14,32,128]{2,1,0:T(8,128)S(1)}, u32[]{:S(2)}, u32[]{:S(2)}) collective-permute-start(f32[14,32,128]{2,1,0:T(8,128)S(1)} %shard_map.48.after), channel_id=1, source_target_pairs={{0,16},{1,17},{2,18},{3,19},{4,20},{5,21},{6,22},{7,23},{8,24},{9,... | collective-permute-start | bytes 688136 | tf_op jit(solution)/shard_map/ppermute | solution.py:259
  7.7 6.2 %collective-permute-start.4 = (f32[1,14,32,128]{3,2,1,0:T(8,128)S(1)}, f32[1,14,32,128]{3,2,1,0:T(8,128)S(1)}, u32[]{:S(2)}, u32[]{:S(2)}) collective-permute-start(f32[1,14,32,128]{3,2,1,0:T(8,128)S(1)} %get-tuple-element.42), channel_id=1, source_target_pairs={{0,8},{1,9},{2,10},{3,11},{4,12},{5,13},{6,14},{7,15},{8,0},{9,1},... | collective-permute-start | bytes 688136 | tf_op jit(solution)/shard_map/ppermute | solution.py:259
  9.2 2.4 %collective-permute-start.2 = (f32[1,7,32,128]{3,2,1,0:T(8,128)S(1)}, f32[1,7,32,128]{3,2,1,0:T(8,128)S(1)}, u32[]{:S(2)}, u32[]{:S(2)}) collective-permute-start(f32[1,7,32,128]{3,2,1,0:T(8,128)S(1)} %get-tuple-element.36), channel_id=1, source_target_pairs={{0,8},{1,9},{2,10},{3,11},{4,12},{5,13},{6,14},{7,15},{8,0},{9,1},... | collective-permute-start | bytes 344072 | tf_op jit(solution)/shard_map/ppermute | solution.py:259
  9.7 1.9 %collective-permute-start.3 = (f32[1,7,32,128]{3,2,1,0:T(8,128)S(1)}, f32[1,7,32,128]{3,2,1,0:T(8,128)S(1)}, u32[]{:S(2)}, u32[]{:S(2)}) collective-permute-start(f32[1,7,32,128]{3,2,1,0:T(8,128)S(1)} %get-tuple-element.37), channel_id=1, source_target_pairs={{0,8},{1,9},{2,10},{3,11},{4,12},{5,13},{6,14},{7,15},{8,0},{9,1},... | collective-permute-start | bytes 344072 | tf_op jit(solution)/shard_map/ppermute | solution.py:259
  11.0 8.1 %collective-permute-start.7 = (f32[1,14,32,128]{3,2,1,0:T(8,128)S(1)}, f32[1,14,32,128]{3,2,1,0:T(8,128)S(1)}, u32[]{:S(2)}, u32[]{:S(2)}) collective-permute-start(f32[1,14,32,128]{3,2,1,0:T(8,128)S(1)} %get-tuple-element.45), channel_id=1, source_target_pairs={{0,8},{1,9},{2,10},{3,11},{4,12},{5,13},{6,14},{7,15},{8,0},{9,1},... | collective-permute-start | bytes 688136 | tf_op jit(solution)/shard_map/ppermute | solution.py:259
  11.6 7.6 %collective-permute-start.9 = (f32[6,32,128]{2,1,0:T(8,128)S(1)}, f32[6,32,128]{2,1,0:T(8,128)S(1)}, u32[]{:S(2)}, u32[]{:S(2)}) collective-permute-start(f32[6,32,128]{2,1,0:T(8,128)S(1)} %get-tuple-element.41.refs_2_), channel_id=1, source_target_pairs={{0,16},{1,17},{2,18},{3,19},{4,20},{5,21},{6,22},{7,23},{8,24},{9,... | collective-permute-start | bytes 294920 | tf_op jit(solution)/shard_map/ppermute | solution.py:259
  11.7 9.2 %collective-permute-start.8 = (f32[8,32,128]{2,1,0:T(8,128)S(1)}, f32[8,32,128]{2,1,0:T(8,128)S(1)}, u32[]{:S(2)}, u32[]{:S(2)}) collective-permute-start(f32[8,32,128]{2,1,0:T(8,128)S(1)} %get-tuple-element.46), channel_id=1, source_target_pairs={{0,16},{1,17},{2,18},{3,19},{4,20},{5,21},{6,22},{7,23},{8,24},{9,... | collective-permute-start | bytes 393224 | tf_op jit(solution)/shard_map/ppermute | solution.py:259
  13.9 9.9 %collective-permute-start.6 = (f32[3,2,32,128]{3,2,1,0:T(8,128)S(1)}, f32[3,2,32,128]{3,2,1,0:T(8,128)S(1)}, u32[]{:S(2)}, u32[]{:S(2)}) collective-permute-start(f32[3,2,32,128]{3,2,1,0:T(8,128)S(1)} %get-tuple-element.44.refs_2_), channel_id=1, source_target_pairs={{0,5},{1,6},{2,7},{3,4},{4,3},{5,0},{6,1},{7,2},{8,13},{9,14},{10,... | collective-permute-start | bytes 294920 | tf_op jit(solution)/shard_map/ppermute | solution.py:259
  16.7 9.1 %collective-permute-start.5 = (f32[4,2,32,128]{3,2,1,0:T(8,128)S(1)}, f32[4,2,32,128]{3,2,1,0:T(8,128)S(1)}, u32[]{:S(2)}, u32[]{:S(2)}) collective-permute-start(f32[4,2,32,128]{3,2,1,0:T(8,128)S(1)} %get-tuple-element.43), channel_id=1, source_target_pairs={{0,7},{1,4},{2,5},{3,6},{4,1},{5,2},{6,3},{7,0},{8,15},{9,12},{10,... | collective-permute-start | bytes 393224 | tf_op jit(solution)/shard_map/ppermute | solution.py:259
  19.2 8.2 %collective-permute-start.11 = (f32[3,2,32,128]{3,2,1,0:T(8,128)S(1)}, f32[3,2,32,128]{3,2,1,0:T(8,128)S(1)}, u32[]{:S(2)}, u32[]{:S(2)}) collective-permute-start(f32[3,2,32,128]{3,2,1,0:T(8,128)S(1)} %shard_map.57.refs_2_), channel_id=1, source_target_pairs={{0,5},{1,6},{2,7},{3,4},{4,3},{5,0},{6,1},{7,2},{8,13},{9,14},{10,... | collective-permute-start | bytes 294920 | tf_op jit(solution)/shard_map/ppermute | solution.py:259
  20.9 8.6 %collective-permute-start.10 = (f32[4,2,32,128]{3,2,1,0:T(8,128)S(1)}, f32[4,2,32,128]{3,2,1,0:T(8,128)S(1)}, u32[]{:S(2)}, u32[]{:S(2)}) collective-permute-start(f32[4,2,32,128]{3,2,1,0:T(8,128)S(1)} %shard_map.58), channel_id=1, source_target_pairs={{0,7},{1,4},{2,5},{3,6},{4,1},{5,2},{6,3},{7,0},{8,15},{9,12},{10,... | collective-permute-start | bytes 393224 | tf_op jit(solution)/shard_map/ppermute | solution.py:259
